TPU v7x, 32 devices: a whole 2x2x4 slice. The times are simulated.
32 devices in a mesh: rep: 2 (over x), fsdp: 4 (over z), seq: 4 (over y, core).
Axes of the slice: x: 2, y: 2, z: 4, core: 2. Of those that a mesh axis runs over, the one named last changes fastest.
Arguments:
- frames: bfloat16 [16, 1536, 768], P(('rep', 'fsdp'), 'seq'), may hold values from -6 to 6
- lengths: int32 [16], P(('rep', 'fsdp')), may hold values from 1152 to 1536, as said below
- cotangent: bfloat16 [16, 1536, 768], P(('rep', 'fsdp'), 'seq')
- dense_in: float32 [2, 768, 6144], P(None, ('fsdp', 'seq'))
- dense_out: float32 [2, 3072, 768], P(None, ('fsdp', 'seq')), may hold values from -0.109375 to 0.109375
- small_params: float32 [2, 12, 768], P(None, None, ('fsdp', 'seq'))
- first_in: float32 [2, 768, 6144], P(None, ('fsdp', 'seq'))
- first_out: float32 [2, 3072, 768], P(None, ('fsdp', 'seq'))
- first_small: float32 [2, 12, 768], P(None, None, ('fsdp', 'seq'))
- second_in: float32 [2, 768, 6144], P(None, ('fsdp', 'seq')), as said below
- second_out: float32 [2, 3072, 768], P(None, ('fsdp', 'seq')), as said below
- second_small: float32 [2, 12, 768], P(None, None, ('fsdp', 'seq')), as said below
Outputs:
- encoded: bfloat16 [16, 1536, 768], P(('rep', 'fsdp'), 'seq')
- frames_grad: float32 [16, 1536, 768], P(('rep', 'fsdp'), 'seq')
- grad_in: float32 [2, 768, 6144], P(None, ('fsdp', 'seq'))
- grad_out: float32 [2, 3072, 768], P(None, ('fsdp', 'seq'))
- grad_small: float32 [2, 12, 768], P(None, None, ('fsdp', 'seq'))
- moment_in: float32 [2, 768, 6144], P(None, ('fsdp', 'seq'))
- moment_out: float32 [2, 3072, 768], P(None, ('fsdp', 'seq'))
- moment_small: float32 [2, 12, 768], P(None, None, ('fsdp', 'seq'))
- square_in: float32 [2, 768, 6144], P(None, ('fsdp', 'seq'))
- square_out: float32 [2, 3072, 768], P(None, ('fsdp', 'seq'))
- square_small: float32 [2, 12, 768], P(None, None, ('fsdp', 'seq'))
- updated_in: float32 [2, 768, 6144], P(None, ('fsdp', 'seq'))
- updated_out: float32 [2, 3072, 768], P(None, ('fsdp', 'seq'))
- updated_small: float32 [2, 12, 768], P(None, None, ('fsdp', 'seq'))
Inputs may be any that keep to these rules, and one draw needn't show every extreme that they name: `lengths`: counted from the start of the clip; of the 2 clips of each (rep, fsdp) pair one has exactly 1536. `second_in`: positive. `second_out`: positive. `second_small`: positive.
All inputs are finite; a program needn't handle non-finite values.
Results may differ from a plain program's by a relative error of at most 0.017.
The roundings to bfloat16 on the way count: a program that leaves them out, or rounds other values in their place, can miss the bound.
Values may be sent and summed in bfloat16 or wider, within the bound.
No kernel may reach another device: no remote copies, remote signals or barrier semaphores. Data moves between devices by JAX's collectives and lax.ppermute only.
A program may use at most 576 MiB of HBM per device.

v0:
```python
import functools
import math

import jax
import jax.numpy as jnp
from jax import lax
from jax.experimental import pallas as pl
from jax.experimental.pallas import tpu as pltpu
from jax.sharding import PartitionSpec as P

HDIM = 64
STEP = 10

NORM_EPSILON = 1e-05
BETA_ONE = 0.9
BETA_TWO = 0.999
ADAM_EPSILON = 1e-08
DECAY_RATE = 0.01
RATE_DENSE = 0.1
RATE_OUTER = 0.05
RATE_SMALL = 0.5
INV_ROOT_TWO = 0.7071067811865476
INV_ROOT_TAU = 0.3989422804014327
LOGIT_SCALE = 0.125
MASKED = -1e30
LANES = 128
VMEM_LIMIT = 60 * 2**20

F32 = jnp.float32
LOW = jnp.bfloat16


def adam_step(weight, gradient, first, second, rate):
    moment = BETA_ONE * first + (1.0 - BETA_ONE) * gradient
    square = BETA_TWO * second + (1.0 - BETA_TWO) * gradient * gradient
    moment_hat = moment / (1.0 - BETA_ONE**STEP)
    square_hat = square / (1.0 - BETA_TWO**STEP)
    updated = weight - rate * (
        moment_hat / (jnp.sqrt(square_hat) + ADAM_EPSILON) + DECAY_RATE * weight
    )
    return (moment, square, updated)


def product(left_side, right_side):
    return jnp.dot(left_side, right_side, preferred_element_type=F32)


def back_product(left_side, right_side):
    return lax.dot_general(
        left_side, right_side, (((1,), (1,)), ((), ())), preferred_element_type=F32
    )


def outer_sum(left_side, right_side):
    return lax.dot_general(
        left_side, right_side, (((0,), (0,)), ((), ())), preferred_element_type=F32
    )


def normalise(values_in):
    centred = values_in - jnp.mean(values_in, axis=-1, keepdims=True)
    scale_inv = lax.rsqrt(jnp.mean(centred * centred, axis=-1, keepdims=True) + NORM_EPSILON)
    return centred * scale_inv, scale_inv


def norm_backward(upstream, gain_row, normal, scale_inv):
    scaled = upstream * gain_row
    inside = (
        scaled
        - jnp.mean(scaled, axis=-1, keepdims=True)
        - normal * jnp.mean(scaled * normal, axis=-1, keepdims=True)
    )
    return (
        scale_inv * inside,
        jnp.sum(upstream * normal, axis=0, keepdims=True),
        jnp.sum(upstream, axis=0, keepdims=True),
    )


def run(kernel, name, steps, ins, outs, scratch, flops, after=(), scalar=None, reuse=()):
    in_arrays, in_specs = zip(*ins)
    out_shapes, out_specs = zip(*outs)
    moved = sum(a.size * a.dtype.itemsize for a in in_arrays)
    moved += sum(math.prod(s.shape) * s.dtype.itemsize for s in out_shapes)
    lead = 0 if scalar is None else 1

    spare = [*after, *reuse]
    aliases = {lead + len(ins) + len(after) + number: number for number in range(len(reuse))}

    def body(*refs):
        kernel(*refs[: lead + len(ins)], *refs[lead + len(ins) + len(spare) :])

    grid_spec = pltpu.PrefetchScalarGridSpec(
        num_scalar_prefetch=lead,
        grid=(steps,),
        in_specs=list(in_specs) + [pl.BlockSpec(memory_space=pl.ANY)] * len(spare),
        out_specs=list(out_specs),
        scratch_shapes=scratch,
    )
    return pl.pallas_call(
        body,
        grid_spec=grid_spec,
        out_shape=list(out_shapes),
        input_output_aliases=aliases,
        compiler_params=pltpu.CompilerParams(vmem_limit_bytes=VMEM_LIMIT),
        cost_estimate=pl.CostEstimate(flops=flops, bytes_accessed=moved, transcendentals=0),
        name=name,
    )(*(() if scalar is None else (scalar,)), *in_arrays, *spare)


def full(shape):
    return pl.BlockSpec(shape, lambda step, *_: (0,) * len(shape))


def scalars():
    return pl.BlockSpec(memory_space=pltpu.SMEM)


def unit_spec(chunk, block, unit_of):
    owners, _, width = chunk.shape
    return chunk, pl.BlockSpec((owners, block, width), lambda step, *_: (0, unit_of(step), 0))


def unit_of_ref(ref):
    return ref[...].reshape(-1, ref.shape[-1])


class Wide:
    def __init__(self, chunk, sent, info, block, units):
        self.chunk, self.sent, self.info = chunk, sent, info
        self.block, self.units = block, units
        self.held = units // 2 if sent else units
        self.mix_at = 2 * self.held
        self.thin_at = self.mix_at + 1

    def mix_spec(self):
        return unit_spec(self.chunk, self.block, lambda step: self.mix_at)

    def inner_specs(self, unit_of):
        arrays = (self.chunk, *self.sent[0]) if self.sent else (self.chunk,)
        return [
            unit_spec(array, self.block, lambda step: lax.rem(unit_of(step), self.held))
            for array in arrays
        ]

    def inner_scratch(self):
        owners, _, width = self.chunk.shape
        return [pltpu.VMEM((owners, self.block, width), LOW)] if self.sent else []

    def outer_specs(self, steps):
        owners, _, width = self.chunk.shape
        if owners == 1:
            return [unit_spec(self.chunk, self.block, lambda step: self.units + step)]
        shape = (owners // steps, self.held * self.block, width)
        specs = [(self.chunk, pl.BlockSpec(shape, lambda step, *_: (step, 1, 0)))]
        if self.sent:
            near = pl.BlockSpec(shape, lambda step, *_: (lax.rem(step, steps // 2), 0, 0))
            specs += [(array, near) for array in self.sent[1]]
        return specs

    def outer_scratch(self, steps):
        owners, _, width = self.chunk.shape
        shape = (owners // steps, self.units * self.block, width)
        return [pltpu.VMEM(shape, LOW)] if self.sent else []

    def count(self):
        return 3 if self.sent else 1


def inner_unit(info_ref, refs, held, half):
    if len(refs) == 1:
        return unit_of_ref(refs[0])
    mine_ref, near_ref, far_ref = refs
    count = near_ref.shape[0]

    @pl.when(info_ref[0] == half)
    def _():
        held[...] = mine_ref[...]

    for core in range(2):

        @pl.when((info_ref[0] != half) & (info_ref[1] == core))
        def _():
            held[core * count : (core + 1) * count] = near_ref[...]
            held[(1 - core) * count : (2 - core) * count] = far_ref[...]

    return unit_of_ref(held)


def outer_unit(info_ref, refs, held, step, steps):
    if len(refs) == 1:
        return unit_of_ref(refs[0])
    mine_ref, near_ref, far_ref = refs
    count = mine_ref.shape[1]
    is_near = step // (steps // 2) == info_ref[1]
    for rep in range(2):

        @pl.when(info_ref[0] == rep)
        def _():
            held[:, rep * count : (rep + 1) * count] = mine_ref[...]

        for ref, wanted in ((near_ref, is_near), (far_ref, jnp.logical_not(is_near))):

            @pl.when((info_ref[0] == rep) & wanted)
            def _():
                held[:, (1 - rep) * count : (2 - rep) * count] = ref[...]

    return unit_of_ref(held)


def project_kernel(hidden_ref, params_ref, unit_ref, normed_ref, q_ref, kv_ref):
    step = pl.program_id(0)

    @pl.when(step == 0)
    def _():
        normal, _ = normalise(hidden_ref[...])
        normed_ref[...] = (normal * params_ref[0:1] + params_ref[1:2]).astype(LOW)

    weights = unit_of_ref(unit_ref)
    added = jnp.where(step == 0, params_ref[2:3], params_ref[3:4])
    added = jnp.where(step == 1, jnp.zeros_like(added), added)
    result = (product(normed_ref[...], weights) + added).astype(LOW)

    @pl.when(step == 0)
    def _():
        q_ref[...] = result

    @pl.when(step > 0)
    def _():
        kv_ref[...] = result


def project(hidden, params, chunk, block, first, after):
    rows, width = hidden.shape
    return run(
        project_kernel,
        "project",
        3,
        [
            (hidden, full(hidden.shape)),
            (params, full(params.shape)),
            unit_spec(chunk, block, lambda step: first + step),
        ],
        [
            (jax.ShapeDtypeStruct((rows, width), LOW), full((rows, width))),
            (jax.ShapeDtypeStruct((rows, width), LOW), full((rows, width))),
            (
                jax.ShapeDtypeStruct((rows, 2 * width), LOW),
                pl.BlockSpec((rows, width), lambda step, *_: (0, jnp.maximum(step - 1, 0))),
            ),
        ],
        [],
        6 * rows * width * width,
        after,
    )


def inner_kernel(count, per_half, info_ref, hidden_ref, mixed_ref, params_ref, mix_ref, *refs):
    unit_refs, refs = refs[:count], refs[count:]
    middle_ref, second_ref, active_ref, slope_ref, *held = refs
    step = pl.program_id(0)

    @pl.when(step == 0)
    def _():
        middle = hidden_ref[...] + (product(mixed_ref[...], unit_of_ref(mix_ref)) + params_ref[4:5])
        middle_ref[...] = middle
        normal, _ = normalise(middle)
        second_ref[...] = (normal * params_ref[5:6] + params_ref[6:7]).astype(LOW)

    @pl.when(step > 0)
    def _():
        weights = inner_unit(info_ref, unit_refs, held[0] if held else None, (step - 1) // per_half)
        inner = product(second_ref[...], weights) + params_ref[pl.ds(step + 7, 1), :]
        cumulative = 0.5 * (1.0 + lax.erf(inner * INV_ROOT_TWO))
        active_ref[...] = (inner * cumulative).astype(LOW)
        slope = cumulative + inner * jnp.exp(-0.5 * inner * inner) * INV_ROOT_TAU
        slope_ref[...] = slope.astype(LOW)


def inner(hidden, mixed_out, params, wide, after):
    units = wide.units
    rows, width = hidden.shape
    spread = pl.BlockSpec((rows, width), lambda step, *_: (0, jnp.maximum(step - 1, 0)))
    return run(
        functools.partial(inner_kernel, wide.count(), max(units // 2, 1)),
        "inner",
        units + 1,
        [
            (wide.info, scalars()),
            (hidden, full(hidden.shape)),
            (mixed_out, full(mixed_out.shape)),
            (params, full(params.shape)),
            wide.mix_spec(),
        ]
        + wide.inner_specs(lambda step: jnp.maximum(step - 1, 0)),
        [
            (jax.ShapeDtypeStruct((rows, width), F32), full((rows, width))),
            (jax.ShapeDtypeStruct((rows, width), LOW), full((rows, width))),
            (jax.ShapeDtypeStruct((rows, units * width), LOW), spread),
            (jax.ShapeDtypeStruct((rows, units * width), LOW), spread),
        ],
        wide.inner_scratch(),
        2 * (units + 1) * rows * width * width,
        after,
    )


def outer_kernel(count, steps, info_ref, middle_ref, active_ref, params_ref, *refs):
    unit_refs, (out_ref, *held) = refs[:count], refs[count:]
    weights = outer_unit(
        info_ref, unit_refs, held[0] if held else None, pl.program_id(0), steps
    )
    term = product(active_ref[...], weights)

    @pl.when(pl.program_id(0) == 0)
    def _():
        out_ref[...] = middle_ref[...] + (term + params_ref[7:8])

    @pl.when(pl.program_id(0) > 0)
    def _():
        out_ref[...] += term


def outer(middle, active, params, wide, steps, after):
    units = wide.units
    rows, width = middle.shape
    return run(
        functools.partial(outer_kernel, wide.count(), steps),
        "outer",
        steps,
        [
            (wide.info, scalars()),
            (middle, full(middle.shape)),
            (active, pl.BlockSpec((rows, units * width // steps), lambda step, *_: (0, step))),
            (params, full(params.shape)),
        ]
        + wide.outer_specs(steps),
        [(jax.ShapeDtypeStruct((rows, width), F32), full((rows, width)))],
        wide.outer_scratch(steps),
        2 * units * rows * width * width,
        after,
    )[0]


def outer_back_kernel(count, steps, info_ref, upstream_ref, slope_ref, *refs):
    unit_refs, refs = refs[:count], refs[count:]
    low_ref, inner_ref, bias_inner_ref, bias_outer_ref, *held = refs
    weights = outer_unit(
        info_ref, unit_refs, held[0] if held else None, pl.program_id(0), steps
    )

    @pl.when(pl.program_id(0) == 0)
    def _():
        low = upstream_ref[...].astype(LOW)
        low_ref[...] = low
        bias_outer_ref[...] = jnp.sum(low.astype(F32), axis=0, keepdims=True)

    grad = (back_product(low_ref[...], weights) * slope_ref[...].astype(F32)).astype(LOW)
    inner_ref[...] = grad
    bias_inner_ref[...] = jnp.sum(grad.astype(F32), axis=0, keepdims=True)


def outer_back(upstream, slope, wide, steps, after):
    units = wide.units
    rows, width = upstream.shape
    share = units * width // steps
    return run(
        functools.partial(outer_back_kernel, wide.count(), steps),
        "outer_back",
        steps,
        [
            (wide.info, scalars()),
            (upstream, full(upstream.shape)),
            (slope, pl.BlockSpec((rows, share), lambda step, *_: (0, step))),
        ]
        + wide.outer_specs(steps),
        [
            (jax.ShapeDtypeStruct((rows, width), LOW), full((rows, width))),
            (
                jax.ShapeDtypeStruct((rows, units * width), LOW),
                pl.BlockSpec((rows, share), lambda step, *_: (0, step)),
            ),
            (
                jax.ShapeDtypeStruct((1, units * width), F32),
                pl.BlockSpec((1, share), lambda step, *_: (0, step)),
            ),
            (jax.ShapeDtypeStruct((1, width), F32), full((1, width))),
        ],
        wide.outer_scratch(steps),
        2 * units * rows * width * width,
        after,
    )


def inner_back_kernel(
    count, units, info_ref, inner_ref, upstream_ref, middle_ref, params_ref, mix_ref, *refs
):
    unit_refs, refs = refs[:count], refs[count:]
    middle_grad_ref, low_ref, mixed_grad_ref, sums_ref, total, *held = refs
    step = pl.program_id(0)

    @pl.when(step == 0)
    def _():
        total[...] = jnp.zeros_like(total)

    @pl.when(step < units)
    def _():
        weights = inner_unit(
            info_ref, unit_refs, held[0] if held else None, step // max(units // 2, 1)
        )
        total[...] += back_product(inner_ref[...], weights)

    @pl.when(step == units)
    def _():
        normal, scale_inv = normalise(middle_ref[...])
        lifted, gain, shift = norm_backward(total[...], params_ref[5:6], normal, scale_inv)
        middle_grad = upstream_ref[...] + lifted
        middle_grad_ref[...] = middle_grad
        low = middle_grad.astype(LOW)
        low_ref[...] = low
        sums_ref[0:1] = gain
        sums_ref[1:2] = shift
        sums_ref[2:3] = jnp.sum(low.astype(F32), axis=0, keepdims=True)
        sums_ref[3:8] = jnp.zeros((5, sums_ref.shape[1]), F32)
        mixed_grad_ref[...] = back_product(low, unit_of_ref(mix_ref)).astype(LOW)


def inner_back(inner_grad, upstream, middle, params, wide, after):
    units = wide.units
    rows, width = upstream.shape
    return run(
        functools.partial(inner_back_kernel, wide.count(), units),
        "inner_back",
        units + 1,
        [
            (wide.info, scalars()),
            (
                inner_grad,
                pl.BlockSpec((rows, width), lambda step, *_: (0, jnp.minimum(step, units - 1))),
            ),
            (upstream, full(upstream.shape)),
            (middle, full(middle.shape)),
            (params, full(params.shape)),
            wide.mix_spec(),
        ]
        + wide.inner_specs(lambda step: jnp.minimum(step, units - 1)),
        [
            (jax.ShapeDtypeStruct((rows, width), F32), full((rows, width))),
            (jax.ShapeDtypeStruct((rows, width), LOW), full((rows, width))),
            (jax.ShapeDtypeStruct((rows, width), LOW), full((rows, width))),
            (jax.ShapeDtypeStruct((8, width), F32), full((8, width))),
        ],
        [pltpu.VMEM((rows, width), F32)] + wide.inner_scratch(),
        2 * (units + 1) * rows * width * width,
        after,
    )


def joined(terms, groups):
    columns = []
    for group in range(groups):
        term = terms[group][...]
        if len(terms) > groups:
            others = terms[groups + group :: groups]
            term = sum([other[...].astype(F32) for other in others], term.astype(F32))
        columns.append(term.astype(LOW))
    return jnp.concatenate(columns, axis=1)


def split_terms(refs, counts):
    groups, parts = counts
    ends = (groups, groups * (parts + 1), groups * (2 * parts + 1))
    return [refs[: ends[0]], refs[ends[0] : ends[1]], refs[ends[1] : ends[2]]], refs[ends[2] :]


def project_back_kernel(counts, hidden_ref, middle_grad_ref, params_ref, *refs):
    terms, (unit_ref, out_ref, sums_ref, total) = split_terms(refs, counts)
    step = pl.program_id(0)
    weights = unit_of_ref(unit_ref)

    @pl.when(step == 0)
    def _():
        grad = joined(terms[0], counts[0])
        sums_ref[2:3] = jnp.sum(grad.astype(F32), axis=0, keepdims=True)
        total[...] = back_product(grad, weights)

    @pl.when(step == 1)
    def _():
        total[...] += back_product(joined(terms[1], counts[0]), weights)

    @pl.when(step == 2)
    def _():
        grad = joined(terms[2], counts[0])
        sums_ref[3:4] = jnp.sum(grad.astype(F32), axis=0, keepdims=True)
        first_grad = total[...] + back_product(grad, weights)
        normal, scale_inv = normalise(hidden_ref[...])
        lowered, gain, shift = norm_backward(first_grad, params_ref[0:1], normal, scale_inv)
        out_ref[...] = middle_grad_ref[...] + lowered
        sums_ref[0:1] = gain
        sums_ref[1:2] = shift
        sums_ref[4:8] = jnp.zeros((4, sums_ref.shape[1]), F32)


def project_back(hidden, middle_grad, params, terms, chunk, block, first, after):
    rows, width = hidden.shape
    whole = full((rows, width))
    counts = (len(terms[0]), len(terms[1]) // len(terms[0]))
    return run(
        functools.partial(project_back_kernel, counts),
        "project_back",
        3,
        [
            (hidden, whole),
            (middle_grad, whole),
            (params, full(params.shape)),
        ]
        + [(term, full(term.shape)) for some in terms for term in some]
        + [unit_spec(chunk, block, lambda step: first + step)],
        [
            (jax.ShapeDtypeStruct((rows, width), F32), whole),
            (jax.ShapeDtypeStruct((8, width), F32), full((8, width))),
        ],
        [pltpu.VMEM((rows, width), F32)],
        6 * rows * width * width,
        after,
    )


def grad_out(cut, units, width):
    if cut is None:
        shape, scratch = (units, width, width), []
        outs = [
            (
                jax.ShapeDtypeStruct(shape, LOW),
                pl.BlockSpec((1, width, width), lambda step, *_: (step, 0, 0)),
            )
        ]
    else:
        far, deep, block = cut
        shape = (far, deep, units, block, width)
        outs = [(jax.ShapeDtypeStruct(shape, LOW), full(shape))] * 2
        scratch = [pltpu.VMEM((deep, 2 * far, block, width), LOW)]
    return outs, scratch


def split_unit(targets_ref, result, refs, unit):
    if len(refs) == 1:
        refs[0][0] = result.astype(LOW)
        return
    keep_ref, give_ref, held = refs
    held[...] = result.astype(LOW).reshape(held.shape)
    far = keep_ref.shape[0]
    for near in range(far):
        keep_ref[near, :, unit] = held[:, targets_ref[near]]
        give_ref[near, :, unit] = held[:, targets_ref[far + near]]


def wide_grad_kernel(units, targets_ref, second_ref, inner_ref, active_ref, low_ref, *refs):
    step = pl.program_id(0)

    @pl.when(step < units)
    def _():
        split_unit(targets_ref, outer_sum(second_ref[...], inner_ref[...]), refs[:3], step)

    @pl.when(step >= units)
    def _():
        result = outer_sum(active_ref[...], low_ref[...])
        if len(refs) == 1:
            refs[0][0] = result.astype(LOW)
        else:
            keep_ref, give_ref, _, held = refs
            held[...] = result.astype(LOW).reshape(held.shape)
            far = keep_ref.shape[0]
            for near in range(far):
                keep_ref[near, step - units] = held[targets_ref[near]]
                give_ref[near, step - units] = held[targets_ref[far + near]]


def wide_weight_grad(cut, targets, second_low, inner_grad, active, outer_low, units, after):
    rows, width = second_low.shape
    outs, scratch = grad_out(cut, 2 * units, width)
    steps = units
    if cut is not None:
        far, steps, block = cut
        shape = (far, steps, 2 * units, block, width)
        spec = pl.BlockSpec(
            (far, steps, units, block, width),
            lambda step, *_: (0, 0, jnp.where(step < units, 0, 1), 0, 0),
        )
        outs = [(jax.ShapeDtypeStruct(shape, LOW), spec)] * 2
        scratch = scratch + [pltpu.VMEM((2 * far, units, block, width), LOW)]
    share = units * width // steps
    return run(
        functools.partial(wide_grad_kernel, units),
        "wide_weight_grad",
        units + steps,
        [
            (targets, scalars()),
            (second_low, full((rows, width))),
            (
                inner_grad,
                pl.BlockSpec((rows, width), lambda step, *_: (0, jnp.minimum(step, units - 1))),
            ),
            (
                active,
                pl.BlockSpec((rows, share), lambda step, *_: (0, jnp.maximum(step - units, 0))),
            ),
            (outer_low, full((rows, width))),
        ],
        outs,
        scratch,
        4 * units * rows * width * width,
        after,
    )


def thin_grad_kernel(counts, targets_ref, normed_ref, mixed_ref, low_ref, *refs):
    terms, refs = split_terms(refs, counts)
    step = pl.program_id(0)
    for number in range(3):

        @pl.when(step == number)
        def _():
            grad = joined(terms[number], counts[0])
            split_unit(targets_ref, outer_sum(normed_ref[...], grad), refs, step)

    @pl.when(step == 3)
    def _():
        split_unit(targets_ref, outer_sum(mixed_ref[...], low_ref[...]), refs, step)


def thin_weight_grad(cut, targets, normed_low, terms, mixed_out, branch_low, after):
    rows, width = normed_low.shape
    outs, scratch = grad_out(cut, 4, width)
    whole = full((rows, width))
    counts = (len(terms[0]), len(terms[1]) // len(terms[0]))
    return run(
        functools.partial(thin_grad_kernel, counts),
        "thin_weight_grad",
        4,
        [
            (targets, scalars()),
            (normed_low, whole),
            (mixed_out, whole),
            (branch_low, whole),
        ]
        + [(term, full(term.shape)) for some in terms for term in some],
        outs,
        scratch,
        8 * rows * width * width,
        after,
    )


def sum_along_kernel(keep_ref, taken_ref, out_ref):
    out_ref[...] = keep_ref[0] + taken_ref[0]


def sum_along(keep, taken, step_far, after):
    _, deep, units, block, width = keep.shape
    spec = pl.BlockSpec(
        (1, 1, units, block, width), lambda step, *_: (step_far, step, 0, 0, 0)
    )
    return run(
        sum_along_kernel,
        "sum_along",
        deep,
        [(keep, spec), (taken, spec)],
        [
            (
                jax.ShapeDtypeStruct((deep, units, block, width), LOW),
                pl.BlockSpec((1, units, block, width), lambda step, *_: (step, 0, 0, 0)),
            )
        ],
        [],
        2 * units * deep * block * width,
        after,
    )[0]


def sum_near_kernel(keep_ref, taken_ref, *refs):
    along, out_ref = refs[:-1], refs[-1]
    total = keep_ref[0].astype(F32) + taken_ref[0].astype(F32)
    for ref in along:
        total += ref[...].astype(F32)
    out_ref[...] = total.astype(LOW)


def sum_near(keep, taken, along, after):
    _, deep, units, block, width = keep.shape
    near = pl.BlockSpec((1, 1, units, block, width), lambda step, *_: (0, step, 0, 0, 0))
    spec = pl.BlockSpec((1, units, block, width), lambda step, *_: (step, 0, 0, 0))
    return run(
        sum_near_kernel,
        "sum_near",
        deep,
        [(keep, near), (taken, near)] + [(array, spec) for array in along],
        [(jax.ShapeDtypeStruct((deep, units, block, width), LOW), spec)],
        [],
        3 * units * deep * block * width,
        after,
    )[0]


def pack_kernel(units, halves, rep_ref, in_ref, rows_ref, *refs):
    out_ref = refs[-1]
    block, width = in_ref.shape[1], out_ref.shape[1]
    count = units // halves

    def column(unit):
        return in_ref[0, :, unit * width : (unit + 1) * width].astype(LOW)

    for half in range(halves):

        @pl.when((rep_ref[0] == half) | (halves == 1))
        def _():
            for unit in range(count):
                out_ref[unit * block : (unit + 1) * block] = column(4 + half * count + unit)
            rows = rows_ref[0, half * count * block : (half + 1) * count * block]
            out_ref[count * block : 2 * count * block] = rows.astype(LOW)

    for number, unit in enumerate((3, 0, 1, 2)):
        at = (2 * count + number) * block
        out_ref[at : at + block] = column(unit)
    if len(refs) > 1:
        out_ref[(2 * count + 4) * block :] = refs[0][...]


def pack(dense_in, dense_out, layer, units, halves, rep, extra, after):
    _, block, columns = dense_in.shape
    width = dense_out.shape[2]
    rows = (2 * units // halves + 4) * block
    ins = [
        (rep, scalars()),
        (dense_in, pl.BlockSpec((1, block, columns), lambda step, *_: (layer, 0, 0))),
        (
            dense_out,
            pl.BlockSpec((1,) + dense_out.shape[1:], lambda step, *_: (layer, 0, 0)),
        ),
    ]
    if extra is not None:
        ins.append((extra, full(extra.shape)))
        rows += extra.shape[0]
    return run(
        functools.partial(pack_kernel, units, halves),
        "pack",
        1,
        ins,
        [(jax.ShapeDtypeStruct((rows, width), LOW), full((rows, width)))],
        [],
        rows * width,
        after,
    )[0]


def small_cut_kernel(layers, block, targets_ref, *refs):
    keep_ref, give_ref, held = refs[-3:]
    _, deep, rows, _ = keep_ref.shape
    each = rows // layers
    keep_ref[...] = jnp.zeros_like(keep_ref)
    give_ref[...] = jnp.zeros_like(give_ref)
    for layer in range(layers):
        one, two, outer_sums, inner_sums = (ref[...] for ref in refs[4 * layer : 4 * layer + 4])
        width = one.shape[1]
        at = layer * each
        held[at : at + 4] = one[:4]
        held[at + 4 : at + 5] = two[2:3]
        held[at + 5 : at + 7] = two[:2]
        held[at + 7 : at + 8] = outer_sums
        for unit in range(each - 8):
            held[at + 8 + unit : at + 9 + unit] = inner_sums[:, unit * width : (unit + 1) * width]
    far = keep_ref.shape[0]
    for depth in range(deep):
        for near in range(far):
            for place in range(2 * far):
                start = (depth * 2 * far + place) * block

                @pl.when(targets_ref[near] == place)
                def _():
                    keep_ref[near, depth, :, :block] = held[:, start : start + block]

                @pl.when(targets_ref[far + near] == place)
                def _():
                    give_ref[near, depth, :, :block] = held[:, start : start + block]


def small_cut(cut, targets, parts, layers, after):
    far, deep, block = cut
    width = parts[0].shape[1]
    rows = layers * (8 + parts[3].shape[1] // width)
    shape = (far, deep, rows, LANES)
    return run(
        functools.partial(small_cut_kernel, layers, block),
        "small_cut",
        1,
        [(targets, scalars())] + [(part, full(part.shape)) for part in parts],
        [(jax.ShapeDtypeStruct(shape, F32), full(shape))] * 2,
        [pltpu.VMEM((rows, width), F32)],
        rows * width,
        after,
    )


def adam_kernel(usual, special, chosen, weight_ref, first_ref, second_ref, *refs):
    grads, (grad_ref, moment_ref, square_ref, updated_ref) = refs[:-4], refs[-4:]
    grad = sum([ref[0].astype(F32) for ref in grads[1:]], grads[0][0].astype(F32))
    grad = grad.reshape(weight_ref.shape)
    rate = jnp.where(pl.program_id(0) == chosen, special, usual)
    moment, square, updated = adam_step(weight_ref[...], grad, first_ref[...], second_ref[...], rate)
    grad_ref[...] = grad
    moment_ref[...] = moment
    square_ref[...] = square
    updated_ref[...] = updated


def adam(state, grads, layer, first, count, from_unit, rates, after, reuse):
    weight = state[0]
    block, width = grads[0].shape[1:]
    if weight.ndim == 3 and weight.shape[2] == width:
        spec = pl.BlockSpec((1, block, width), lambda step, *_: (layer, first + step, 0))
    elif weight.ndim == 3:
        spec = pl.BlockSpec((1, block, width), lambda step, *_: (layer, 0, first + step))
    else:
        spec = pl.BlockSpec((1, 1, block, width), lambda step, *_: (layer, first + step, 0, 0))
    usual, special, chosen = rates
    return run(
        functools.partial(adam_kernel, usual, special, chosen - first),
        "adam",
        count,
        [(array, spec) for array in state]
        + [
            (grad, pl.BlockSpec((1, block, width), lambda step, *_: (from_unit + step, 0, 0)))
            for grad in grads
        ],
        [(jax.ShapeDtypeStruct(weight.shape, F32), spec)] * 4,
        [],
        16 * count * block * width,
        after,
        None,
        reuse,
    )


def part_kernel(lower_ref, rows_ref, keep_ref, give_ref):
    count = keep_ref.shape[0]
    lower, upper = rows_ref[:count], rows_ref[count:]
    in_lower = lower_ref[0] != 0
    keep_ref[...] = jnp.where(in_lower, lower, upper).astype(keep_ref.dtype)
    give_ref[...] = jnp.where(in_lower, upper, lower).astype(LOW)


def part_clips(in_lower, rows, kind, after):
    count, width = rows.shape[0] // 2, rows.shape[1]
    return run(
        part_kernel,
        "part_clips",
        1,
        [(in_lower, scalars()), (rows, full(rows.shape))],
        [
            (jax.ShapeDtypeStruct((count, width), kind), full((count, width))),
            (jax.ShapeDtypeStruct((count, width), LOW), full((count, width))),
        ],
        [],
        rows.size,
        after,
    )


def query_block(rows):
    return next(size for size in (768, 384, 256, 128) if rows % size == 0)


def attend_kernel(parts, block, bias_ref, q_ref, *refs):
    k_refs, v_refs = refs[:parts], refs[parts : 2 * parts]
    o_ref, lse_ref = refs[2 * parts :]
    rows = q_ref.shape[0]
    q_side = (q_ref[...] * jnp.bfloat16(LOGIT_SCALE)).T
    ones = jnp.ones((16, rows), LOW)
    v_heads = []
    for ref in v_refs:
        side = ref[...].T
        v_heads.append(
            [jnp.concatenate([side[h * HDIM : (h + 1) * HDIM], ones]) for h in range(2)]
        )
    head_of = lax.broadcasted_iota(jnp.int32, (LANES, block), 0) // HDIM
    for start in range(0, rows, block):
        q_block = q_side[:, start : start + block]
        both = []
        for head in range(2):
            q_head = jnp.where(head_of == head, q_block, jnp.zeros_like(q_block))
            scores = []
            for part in range(parts):
                score = product(k_refs[part][...], q_head)
                lower, upper = score[: rows // 2], score[rows // 2 :]
                bias = jnp.tile(bias_ref[part], (1, block // LANES))
                scores.append(jnp.concatenate([lower, upper + bias], axis=0))
            top = functools.reduce(
                jnp.maximum, [jnp.max(score, axis=0, keepdims=True) for score in scores]
            )
            weights = [jnp.exp(score - top).astype(LOW) for score in scores]
            summed = sum(product(v_heads[part][head], weights[part]) for part in range(parts))
            total = summed[HDIM : HDIM + 1]
            both.append(summed[:HDIM] / total)
            lse_ref[0, head : head + 1, start : start + block] = top + jnp.log(total)
        o_ref[start : start + block, :] = jnp.concatenate(both, axis=0).T.astype(LOW)


def attend(queries, own, others, bias, after):
    rows, width = queries.shape
    pairs = width // LANES
    parts = len(others) + 1

    def columns(base):
        return pl.BlockSpec((rows, LANES), lambda pair, *_: (0, base * pairs + pair))

    return run(
        functools.partial(attend_kernel, parts, query_block(rows)),
        "attend",
        pairs,
        [(bias, full(bias.shape)), (queries, columns(0))]
        + [(array, columns(0)) for array in (own, *others)]
        + [(array, columns(1)) for array in (own, *others)],
        [
            (jax.ShapeDtypeStruct((rows, width), LOW), columns(0)),
            (
                jax.ShapeDtypeStruct((pairs, 2, rows), F32),
                pl.BlockSpec((1, 2, rows), lambda pair, *_: (pair, 0, 0)),
            ),
        ],
        [],
        16 * rows * rows * parts * width,
        after,
    )


def attend_back_kernel(parts, block, bias_ref, q_ref, *refs):
    k_refs, v_refs = refs[:parts], refs[parts : 2 * parts]
    o_ref, do_ref, lse_ref = refs[2 * parts : 2 * parts + 3]
    dq_ref = refs[2 * parts + 3]
    dk_refs = refs[2 * parts + 4 : 3 * parts + 4]
    dv_refs = refs[3 * parts + 4 :]
    rows = q_ref.shape[0]
    q_rows = q_ref[...] * jnp.bfloat16(LOGIT_SCALE)
    do_rows = do_ref[...]
    q_side, do_side = q_rows.T, do_rows.T
    shared = (do_rows.astype(F32) * o_ref[...].astype(F32)).T
    delta = [
        jnp.sum(shared[head * HDIM : (head + 1) * HDIM], axis=0, keepdims=True)
        for head in range(2)
    ]
    head_of = lax.broadcasted_iota(jnp.int32, (LANES, rows), 0) // HDIM
    zeros = jnp.zeros_like(q_side)
    q_heads = [jnp.where(head_of == head, q_side, zeros) for head in range(2)]
    do_heads = [jnp.where(head_of == head, do_side, zeros) for head in range(2)]
    lane = lax.broadcasted_iota(jnp.int32, (block, LANES), 1)
    dq_sides = [jnp.zeros((HDIM, rows), F32)] * 2
    for part in range(parts):
        for start in range(0, rows, block):
            here = slice(start, start + block)
            k_block, v_block = k_refs[part][here], v_refs[part][here]
            k_side = k_block.T
            dk_heads, dv_heads = [], []
            for head in range(2):
                score = product(k_block, q_heads[head])
                if start + block > rows // 2:
                    skip = max(rows // 2 - start, 0)
                    upper = bias_ref[part][start + skip - rows // 2 : start + block - rows // 2]
                    raised = score[skip:] + jnp.tile(upper, (1, rows // LANES))
                    score = jnp.concatenate([score[:skip], raised], axis=0) if skip else raised
                chances = jnp.exp(score - lse_ref[0, head : head + 1])
                chance_grad = product(v_block, do_heads[head])
                score_grad = (chances * (chance_grad - delta[head])).astype(LOW)
                dq_sides[head] = dq_sides[head] + product(
                    k_side[head * HDIM : (head + 1) * HDIM], score_grad
                )
                dk_heads.append(product(score_grad, q_rows))
                dv_heads.append(product(chances.astype(LOW), do_rows))
            dk_refs[part][here] = jnp.where(lane < HDIM, *dk_heads).astype(LOW)
            dv_refs[part][here] = jnp.where(lane < HDIM, *dv_heads).astype(LOW)
    dq_ref[...] = (jnp.concatenate(dq_sides, axis=0) * LOGIT_SCALE).T.astype(LOW)


def attend_back(queries, own, others, mixed_out, mixed_grad, log_total, bias, group, groups, after):
    rows, width = queries.shape
    pairs = width // LANES
    parts = len(others) + 1
    first = group * pairs // groups
    count = (group + 1) * pairs // groups - first

    def columns(base):
        return pl.BlockSpec((rows, LANES), lambda pair, *_: (0, base * pairs + first + pair))

    out = run(
        functools.partial(attend_back_kernel, parts, query_block(rows)),
        "attend_back",
        count,
        [(bias, full(bias.shape)), (queries, columns(0))]
        + [(array, columns(0)) for array in (own, *others)]
        + [(array, columns(1)) for array in (own, *others)]
        + [
            (mixed_out, columns(0)),
            (mixed_grad, columns(0)),
            (log_total, pl.BlockSpec((1, 2, rows), lambda pair, *_: (first + pair, 0, 0))),
        ],
        [
            (
                jax.ShapeDtypeStruct((rows, count * LANES), LOW),
                pl.BlockSpec((rows, LANES), lambda pair, *_: (0, pair)),
            )
        ]
        * (2 * parts + 1),
        [],
        40 * rows * rows * parts * count * LANES,
        after,
    )
    return out[0], out[1 : parts + 1], out[parts + 1 :]


def on_device(
    frames,
    lengths,
    cotangent,
    dense_in,
    dense_out,
    small_params,
    first_in,
    first_out,
    first_small,
    second_in,
    second_out,
    second_small,
):
    clip_count, local_frames, width = frames.shape
    layer_count, block, columns_in = dense_in.shape
    units = columns_in // width - 4
    seq, deep, reps = lax.axis_size("seq"), lax.axis_size("fsdp"), lax.axis_size("rep")
    half = seq // clip_count
    total_frames = local_frames * seq
    place, depth = lax.axis_index("seq"), lax.axis_index("fsdp")
    owners = seq * deep
    my_clip, my_member = place // half, place % half
    in_lower = my_clip == 0
    swap = [(source, (source + half) % seq) for source in range(seq)]
    far = seq // 2
    row, core = place // 2, place % 2
    cut = (far, deep, block) if block % 16 == 0 else None

    def turn(axis, step):
        size = lax.axis_size(axis)
        return [(source, (source + step) % size) for source in range(size)]

    over_core = [(source, source ^ 1) for source in range(seq)]

    def to_clips(arrays):
        whole = jnp.stack(arrays, axis=1)
        kept = lax.dynamic_index_in_dim(whole, my_clip, 0, keepdims=False)
        given = lax.dynamic_index_in_dim(whole, 1 - my_clip, 0, keepdims=False)
        taken = lax.ppermute(given, "seq", swap)
        lower, upper = jnp.where(in_lower, kept, taken), jnp.where(in_lower, taken, kept)
        return [
            jnp.concatenate([lower[number], upper[number]], axis=0).astype(F32)
            for number in range(len(arrays))
        ]

    def split_clips(rows):
        lower, upper = rows[:local_frames], rows[local_frames:]
        return jnp.where(in_lower, lower, upper), jnp.where(in_lower, upper, lower).astype(LOW)

    def from_clips(kept, given):
        taken = lax.ppermute(given, "seq", swap).astype(kept.dtype)
        return jnp.stack([jnp.where(in_lower, kept, taken), jnp.where(in_lower, taken, kept)])

    def around(step):
        return [
            (source, source - source % half + (source % half + step) % half)
            for source in range(seq)
        ]

    halves = 2 if reps == 2 and units % 2 == 0 and deep % 2 == 0 and cut is not None else 1
    info = jnp.stack([lax.axis_index("rep"), core])

    def gather(layer, extra, after):
        if cut is None:
            columns = dense_in[layer].astype(LOW).reshape(block, 4 + units, width)
            columns = columns.transpose(1, 0, 2)
            columns = lax.all_gather(columns, ("fsdp", "seq"), axis=1, tiled=True)
            rows = lax.all_gather(
                dense_out[layer].astype(LOW), ("fsdp", "seq"), axis=0, tiled=True
            )
            parts = [columns[4:].reshape(-1, width), rows, columns[3], *columns[:3]]
            return Wide(jnp.concatenate(parts)[None], None, info, width, units)
        own = pack(dense_in, dense_out, layer, units, halves, info, extra, after)
        chunk = lax.all_gather(own, ("fsdp", "seq"), axis=0)
        if halves == 1:
            return Wide(chunk, None, info, block, units)
        return Wide(chunk, [None, None], info, block, units)

    def share(wide, marker):
        wide.given = []
        if wide.sent:
            wide.chunk, marker = lax.optimization_barrier((wide.chunk, marker))
            rows = units // 2 * block
            shape = (owners // 2, rows, width)
            wide.given = [
                lax.dynamic_slice(wide.chunk, (core * (owners // 2), number * rows, 0), shape)
                for number in range(2)
            ]
            wide.near = [lax.ppermute(part, "rep", turn("rep", 1)) for part in wide.given]
        return marker

    def exchange(wide, number, marker):
        if wide.sent:
            near, marker = lax.optimization_barrier((wide.near[number], marker))
            wide.sent[number] = (near, lax.ppermute(near, "seq", over_core))
        return marker

    targets = jnp.stack(
        [
            (row + step) % far * 2 + (core + other) % 2
            for other in range(2)
            for step in range(far)
        ]
    )

    def start_core(parts):
        if cut is None:
            return parts, []
        return (parts[0], lax.ppermute(parts[1], "seq", over_core)), [parts[0]]

    def start_far(chunk, after):
        if cut is None:
            return chunk
        keep, taken = chunk[0]
        sums = [sum_along(keep, taken, step, after) for step in range(1, far)]
        moved = [
            lax.ppermute(part, "seq", turn("seq", 2 * step + 2)) for step, part in enumerate(sums)
        ]
        return (keep, taken, moved), sums

    def whole_deep(chunk, after):
        if cut is None:
            return chunk
        total = sum_near(*chunk[0], after)
        return lax.psum_scatter(total, "fsdp", scatter_dimension=0, tiled=True)[0], [total]

    def start_reps(chunk):
        if cut is None:
            result = chunk[0][0]
            owned = lax.psum_scatter(
                result[:units], ("fsdp", "seq"), scatter_dimension=1, tiled=True
            )
            if result.shape[0] > units:
                rows = lax.psum_scatter(
                    result[units:].reshape(units * width, width),
                    ("fsdp", "seq"),
                    scatter_dimension=0,
                    tiled=True,
                )
                owned = jnp.concatenate([owned, rows.reshape(units, block, width)])
        else:
            owned = chunk[0]
        return owned, [lax.ppermute(owned, "rep", turn("rep", step)) for step in range(1, reps)]

    def finish(state):
        owned, arrived = state
        return sum([part.astype(F32) for part in arrived], owned.astype(F32))

    length = lax.dynamic_index_in_dim(lengths, my_clip, 0, keepdims=False)
    bias = jnp.stack(
        [
            jnp.broadcast_to(
                jnp.where(
                    (half + (my_member - step) % half) * local_frames
                    + jnp.arange(local_frames, dtype=jnp.int32)
                    < length,
                    0.0,
                    MASKED,
                )[:, None],
                (local_frames, LANES),
            )
            for step in range(half)
        ]
    ).astype(F32)

    small_low = small_params.astype(LOW)
    extra = None
    if cut is not None:
        extra = jnp.pad(small_low.reshape(-1), (0, -small_low.size % (16 * width)))
        extra = extra.reshape(-1, width)
    wides = []
    for layer in range(layer_count):
        wides.append(gather(layer, extra if layer == 0 else None, []))
    if cut is None:
        params_all = lax.all_gather(small_low, ("fsdp", "seq"), axis=2, tiled=True)
    else:
        first_row = (wides[0].thin_at + 3) * block
        params_all = wides[0].chunk[:, first_row:].reshape(owners, -1)[:, : small_low.size]
        params_all = params_all.reshape((owners,) + small_low.shape).transpose(1, 2, 0, 3)
        params_all = params_all.reshape(layer_count, -1, width)
    params_all = params_all.astype(F32)

    row_steps = units if cut is None else deep
    hidden, upstream = to_clips([frames, cotangent])
    stored = []
    for layer_index in range(layer_count):
        params = params_all[layer_index]
        wide = wides[layer_index]
        hidden = share(wide, hidden)
        normed_low, queries, own = project(
            hidden, params, wide.chunk, wide.block, wide.thin_at, wide.given
        )
        others = [lax.ppermute(own, "seq", around(step)) for step in range(1, half)]
        mixed_out, log_total = attend(queries, own, others, bias, [])
        mixed_out = exchange(wide, 0, mixed_out)
        middle, second_low, active, slope = inner(hidden, mixed_out, params, wide, [])
        middle = exchange(wide, 1, middle)
        stored.append(
            (hidden, normed_low, queries, own, others, log_total, mixed_out)
            + (middle, second_low, active, slope)
        )
        if layer_index + 1 < layer_count:
            hidden = outer(middle, active, params, wide, row_steps, [])
    groups = 2 if width // LANES % 2 == 0 else 1
    def arrivals(number):
        return [
            part
            for layer in range(1, layer_count)
            for some in parts_out[layer][number : number + 1]
            for part in some[1]
        ]

    order = []
    waiting = None
    parts_out = {}
    done_in, done_out = (), ()
    rows_shape = (layer_count, units, block, width)
    states_in = (dense_in, first_in, second_in)
    states_out = (dense_out, first_out, second_out)
    if cut is None:
        states_out = [array.reshape(rows_shape) for array in states_out]
    rates_in = (RATE_DENSE, RATE_DENSE * math.sqrt(total_frames / 3.0), 3)
    rates_out = (RATE_OUTER, RATE_OUTER, 0)

    def flat(part):
        return [part[0]] + part[1]

    small_grads = []
    for layer_index in reversed(range(layer_count)):
        wide = wides[layer_index]
        params = params_all[layer_index]
        (
            hidden,
            normed_low,
            queries,
            own,
            others,
            log_total,
            mixed_out,
            middle,
            second_low,
            active,
            slope,
        ) = stored[layer_index]
        outer_low, inner_grad, bias_inner, bias_outer = outer_back(
            upstream, slope, wide, row_steps, order
        )
        order = [inner_grad]
        if waiting:
            waiting = start_far(waiting, order)
            order = order + waiting[1]
        wide_part = start_core(
            wide_weight_grad(
                cut, targets, second_low, inner_grad, active, outer_low, units, order
            )
        )
        middle_grad, branch_low, mixed_grad, sums_two = inner_back(
            inner_grad, upstream, middle, params, wide, wide_part[1]
        )
        order = [middle_grad]
        wide_part = start_far(wide_part, order)
        order = order + wide_part[1]
        q_terms, k_near, v_near, k_far, v_far = [], [], [], [], []
        for group in range(groups):
            q_term, k_terms, v_terms = attend_back(
                queries,
                own,
                others,
                mixed_out,
                mixed_grad,
                log_total,
                bias,
                group,
                groups,
                order,
            )
            q_terms.append(q_term)
            k_near.append(k_terms[0])
            v_near.append(v_terms[0])
            k_far.append(k_terms[1:])
            v_far.append(v_terms[1:])
            order = [q_term]
            if waiting and group == 0:
                waiting = whole_deep(waiting, order)
                order = order + waiting[1]

        def all_terms(near, terms):
            moved = [
                lax.ppermute(terms[group][step - 1], "seq", around(half - step))
                for step in range(1, half)
                for group in range(groups)
            ]
            return list(near) + moved

        terms = [q_terms, all_terms(k_near, k_far), all_terms(v_near, v_far)]
        order = [q_terms[-1]]

        if layer_index == 0:
            if waiting:
                waiting = start_reps(waiting)
                parts_out[1] += (waiting,)
            thin_part = start_core(
                thin_weight_grad(
                    cut, targets, normed_low, terms, mixed_out, branch_low, order
                )
            )
            wide_part = whole_deep(wide_part, thin_part[1] + arrivals(0))
            for layer in reversed(range(1, layer_count)):
                last = flat(parts_out[layer][0])
                done_out = adam(
                    states_out, last, layer, 0, units, units, rates_out, wide_part[1], done_out
                )
            thin_part = start_far(thin_part, list(done_out[:1]) + arrivals(1))
            order = thin_part[1]
        upstream, sums_one = project_back(
            hidden, middle_grad, params, terms, wide.chunk, wide.block, wide.thin_at, order
        )
        if layer_index > 0:
            if waiting:
                waiting = start_reps(waiting)
                parts_out[layer_index + 1] += (waiting,)
            wide_part = whole_deep(wide_part, [upstream])
            thin_part = start_core(
                thin_weight_grad(
                    cut,
                    targets,
                    normed_low,
                    terms,
                    mixed_out,
                    branch_low,
                    [upstream] + wide_part[1],
                )
            )
        waiting = thin_part
        order = waiting[1]
        parts_out[layer_index] = (start_reps(wide_part) if layer_index > 0 else wide_part,)
        small_grads = [sums_one, sums_two, bias_outer, bias_inner] + small_grads
    if cut is not None:
        keep, give = small_cut(cut, targets, small_grads, layer_count, [upstream])
        cuts = keep + lax.ppermute(give, "seq", over_core)
        along = [lax.ppermute(cuts[step], "seq", turn("seq", 2 * step)) for step in range(1, far)]

    middle, active = stored[-1][7], stored[-1][9]
    result = outer(middle, active, params_all[-1], wides[-1], row_steps, [upstream])
    for layer in reversed(range(1, layer_count)):
        last = flat(parts_out[layer][0])
        done_in = adam(states_in, last, layer, 4, units, 0, rates_in, [result], done_in)
    waiting = whole_deep(waiting, list(done_out[:1]) + list(done_in[:1]) + [result])
    order = waiting[1] or [upstream]
    ready = order + (along if cut else [])
    encoded = from_clips(*part_clips(in_lower.astype(jnp.int32).reshape(1), result, LOW, ready))
    for layer in reversed(range(1, layer_count)):
        last = flat(parts_out[layer][1])
        done_in = adam(states_in, last, layer, 0, 4, 0, rates_in, order, done_in)
    wide_part = parts_out[0][0]
    if cut is not None and done_in:
        mine, *done_in = lax.optimization_barrier((wide_part[0], *done_in))
        wide_part = (mine, wide_part[1])
    wide_part = start_reps(wide_part)
    ready = order + list(done_in[:1])
    frames_grad = from_clips(
        *part_clips(in_lower.astype(jnp.int32).reshape(1), upstream, F32, ready)
    )
    if cut is not None:
        total = sum(along, cuts[0])
        deeper = [
            lax.ppermute(
                lax.dynamic_index_in_dim(total, (depth + step) % deep, 0, keepdims=False),
                "fsdp",
                turn("fsdp", step),
            )
            for step in range(1, deep)
        ]
    done_in = adam(states_in, flat(wide_part), 0, 4, units, 0, rates_in, order, done_in)
    thin_part = start_reps(waiting)
    order = order + [done_in[0], thin_part[0]]
    done_out = adam(states_out, flat(wide_part), 0, 0, units, units, rates_out, order, done_out)
    if cut is None:
        small_all = jnp.stack(
            [
                jnp.concatenate([one[:4], two[2:3], two[:2], outer_sums])
                for one, two, outer_sums, _ in zip(*[iter(small_grads)] * 4)
            ]
        )
        inner_all = jnp.stack([part.reshape(units, width) for part in small_grads[3::4]])
        small_all = jnp.concatenate([small_all, inner_all], axis=1)
        small_all = small_all.reshape(layer_count, -1, owners, block).transpose(2, 0, 1, 3)
        owned_small = lax.psum_scatter(
            small_all, ("fsdp", "seq"), scatter_dimension=0, tiled=True
        )
    else:
        (total, *deeper, _) = lax.optimization_barrier((total, *deeper, done_in[0]))
        owned_small = lax.dynamic_index_in_dim(total, depth, 0, keepdims=False)
        owned_small = sum(deeper, owned_small)[:, :block]
    owned_small = owned_small.reshape(small_params.shape).astype(LOW)
    done_in = adam(states_in, flat(thin_part), 0, 0, 4, 0, rates_in, [done_out[0]], done_in)
    grad_in, moment_in, square_in, updated_in = done_in
    grad_out_rows, moment_out, square_out, updated_out = (
        array.reshape(dense_out.shape) for array in done_out
    )
    grad_small = finish(
        (owned_small, [lax.ppermute(owned_small, "rep", turn("rep", s)) for s in range(1, reps)])
    )
    moment_small, square_small, updated_small = adam_step(
        small_params, grad_small, first_small, second_small, RATE_SMALL
    )
    return (
        encoded,
        frames_grad,
        grad_in,
        grad_out_rows,
        grad_small,
        moment_in,
        moment_out,
        moment_small,
        square_in,
        square_out,
        square_small,
        updated_in,
        updated_out,
        updated_small,
    )


def solution(mesh):
    clips = P(("rep", "fsdp"), "seq", None)
    rows = P(None, ("fsdp", "seq"), None)
    lanes = P(None, None, ("fsdp", "seq"))
    return jax.shard_map(
        on_device,
        mesh=mesh,
        in_specs=(clips, P(("rep", "fsdp")), clips) + (rows, rows, lanes) * 3,
        out_specs=(clips, clips) + (rows, rows, lanes) * 4,
        check_vma=False,
    )
```

profile of v0, /device:TPU:0, one launch (start us, length us, event | category | flops | bytes accessed | tf_op | source)
XLA Modules:
  0.0 618.4 jit_solution(16239628100051278776)
XLA Ops:
  9.3 2.4 pack.3
  11.8 2.5 pack.2
  15.5 3.0 collective-permute-start
  18.4 32.8 %collective-permute-done = bf16[2,384,768]{2,1,0:T(8,128)(2,1)S(1)} collective-permute-done((bf16[2,384,768]{2,1,0:T(8,128)(2,1)}, bf16[2,384,768]{2,1,0:T(8,128)(2,1)S(1)}, u32[]{:S(2)}, u32[]{:S(2)}) %collective-permute-start) | collective-permute-done | bytes 1179680 | tf_op jit(solution)/shard_map/ppermute | solution.py:1058
  52.3 1.6 maximum_convert_fusion.refs_0_.refs_1_
  53.9 47.9 %all-gather.7.cloned.1.call-done = bf16[6400,768]{1,0:T(8,128)(2,1)} async-done(((bf16[400,768]{1,0:T(8,128)(2,1)}), bf16[6400,768]{1,0:T(8,128)(2,1)}) %all-gather.7.cloned.1.call-update) | async-done | bytes 9830416 | tf_op jit(solution)/shard_map/all_gather | solution.py:1093
  104.5 3.2 constant_dynamic-slice_fusion.2
  107.7 8.3 %project.2 = (bf16[768,768]{1,0:T(8,128)(2,1)}, bf16[768,768]{1,0:T(8,128)(2,1)}, bf16[768,1536]{1,0:T(8,128)(2,1)}) custom-call(f32[768,768]{1,0:T(8,128)} %maximum_convert_fusion.refs_0_.refs_1_, f32[12,768]{1,0:T(8,128)} %squeeze.68.refs_1_.refs_3_.refs_4_.refs_2_, bf16[16,400,768]{2,1,0:T(8,128)(2,1)} %bitcast.63, ...), custom_call_target="tpu_custom_call" | custom-call | flops 2717908992 | bytes 16945152 | tf_op jit(solution)/shard_map/project/pallas_call | solution.py:100
  118.6 1.6 collective-permute-start.2
  120.9 23.5 %attend.2 = (bf16[768,768]{1,0:T(8,128)(2,1)}, f32[6,2,768]{2,1,0:T(2,128)}) custom-call(f32[2,384,128]{2,1,0:T(8,128)} %pad_maximum_fusion.2.refs_0_, bf16[768,768]{1,0:T(8,128)(2,1)} %get-tuple-element.133.refs_1_, bf16[768,1536]{1,0:T(8,128)(2,1)} %get-tuple-element.134.refs_2_.refs_4_, bf16[768,1536]{1,0:T(8,128)(2,1)} %collective-permute-done.3.refs_3_.refs_5_, ...), custom_call_target="tpu_custom_call" | custom-call | flops 14495514624 | bytes 12226560 | tf_op jit(solution)/shard_map/attend/pallas_call | solution.py:100
  144.4 2.3 collective-permute-done.2.refs_6_.refs_7_
  146.7 1.7 collective-permute-start.1
  149.7 15.6 %inner.2 = (f32[768,768]{1,0:T(8,128)}, bf16[768,768]{1,0:T(8,128)(2,1)}, bf16[768,3072]{1,0:T(8,128)(2,1)}, bf16[768,3072]{1,0:T(8,128)(2,1)}) custom-call(s32[2]{0:T(128)} %pad_add_fusion.refs_0_, f32[768,768]{1,0:T(8,128)} %maximum_convert_fusion.refs_0_.refs_1_, bf16[768,768]{1,0:T(8,128)(2,1)} %get-tuple-element.136.refs_2_.refs_6_, ...), custom_call_target="tpu_custom_call" | custom-call | flops 4529848320 | bytes 38572040 | tf_op jit(solution)/shard_map/inner/pallas_call | solution.py:100
  165.3 9.8 %collective-permute-done.1.refs_5_.refs_4_ = bf16[8,96,768]{2,1,0:T(8,128)(2,1)S(1)} collective-permute-done((bf16[8,96,768]{2,1,0:T(8,128)(2,1)S(1)}, bf16[8,96,768]{2,1,0:T(8,128)(2,1)S(1)}, u32[]{:S(2)}, u32[]{:S(2)}) %collective-permute-start.1) | collective-permute-done | bytes 1179680 | tf_op jit(solution)/shard_map/ppermute | solution.py:1108
  179.1 10.4 %outer.2.refs_0_.refs_1_ = f32[768,768]{1,0:T(8,128)} custom-call(s32[2]{0:T(128)} %pad_add_fusion.refs_0_, f32[768,768]{1,0:T(8,128)} %get-tuple-element.139.refs_1_.refs_3_, bf16[768,3072]{1,0:T(8,128)(2,1)} %get-tuple-element.140.refs_2_.refs_3_, f32[12,768]{1,0:T(8,128)} %squeeze.68.refs_1_.refs_3_.refs_4_.refs_2_, bf16[16,400,768]{2,1,0:T(8,128)(2,1)} %bitcast.66, ...), custom_call_target="tpu_custom_call" | custom-call | flops 3623878656 | bytes 21663752 | tf_op jit(solution)/shard_map/outer/pallas_call | solution.py:100
  189.5 3.3 constant_dynamic-slice_fusion
  192.7 8.7 %project.3 = (bf16[768,768]{1,0:T(8,128)(2,1)}, bf16[768,768]{1,0:T(8,128)(2,1)}, bf16[768,1536]{1,0:T(8,128)(2,1)}) custom-call(f32[768,768]{1,0:T(8,128)} %outer.2.refs_0_.refs_1_, f32[12,768]{1,0:T(8,128)} %squeeze.69.refs_1_.refs_3_.refs_4_.refs_2_, bf16[16,384,768]{2,1,0:T(8,128)(2,1)} %bitcast.72, bf16[8,96,768]{2,1,0:T(8,128)(2,1)} %get-tuple-element.267.refs_3_, ...), custom_call_target="tpu_custom_call" | custom-call | flops 2717908992 | bytes 16551936 | tf_op jit(solution)/shard_map/project/pallas_call | solution.py:100
  203.0 3.2 collective-permute-done.8.refs_3_.refs_5_
  207.7 23.5 %attend.3 = (bf16[768,768]{1,0:T(8,128)(2,1)}, f32[6,2,768]{2,1,0:T(2,128)}) custom-call(f32[2,384,128]{2,1,0:T(8,128)} %pad_maximum_fusion.2.refs_0_, bf16[768,768]{1,0:T(8,128)(2,1)} %get-tuple-element.144.refs_1_, bf16[768,1536]{1,0:T(8,128)(2,1)} %get-tuple-element.145.refs_2_.refs_4_, bf16[768,1536]{1,0:T(8,128)(2,1)} %copy-done.33, ...), custom_call_target="tpu_custom_call" | custom-call | flops 14495514624 | bytes 12226560 | tf_op jit(solution)/shard_map/attend/pallas_call | solution.py:100
  235.2 15.5 %inner.3 = (f32[768,768]{1,0:T(8,128)}, bf16[768,768]{1,0:T(8,128)(2,1)}, bf16[768,3072]{1,0:T(8,128)(2,1)}, bf16[768,3072]{1,0:T(8,128)(2,1)}) custom-call(s32[2]{0:T(128)} %pad_add_fusion.refs_0_, f32[768,768]{1,0:T(8,128)} %outer.2.refs_0_.refs_1_, bf16[768,768]{1,0:T(8,128)(2,1)} %get-tuple-element.147.refs_2_.refs_6_, ...), custom_call_target="tpu_custom_call" | custom-call | flops 4529848320 | bytes 37785608 | tf_op jit(solution)/shard_map/inner/pallas_call | solution.py:100
  250.6 9.1 %collective-permute-done.6.refs_4_.refs_5_ = bf16[8,96,768]{2,1,0:T(8,128)(2,1)} collective-permute-done((bf16[8,96,768]{2,1,0:T(8,128)(2,1)S(1)}, bf16[8,96,768]{2,1,0:T(8,128)(2,1)}, u32[]{:S(2)}, u32[]{:S(2)}) %collective-permute-start.6) | collective-permute-done | bytes 1179680 | tf_op jit(solution)/shard_map/ppermute | solution.py:1108
  260.4 2.6 maximum_convert_fusion.1.refs_1_.refs_2_
  264.0 10.3 %outer_back.2 = (bf16[768,768]{1,0:T(8,128)(2,1)}, bf16[768,3072]{1,0:T(8,128)(2,1)}, f32[1,3072]{1,0:T(1,128)}, f32[1,768]{1,0:T(1,128)}) custom-call(s32[2]{0:T(128)} %pad_add_fusion.refs_0_, f32[768,768]{1,0:T(8,128)} %maximum_convert_fusion.1.refs_1_.refs_2_, bf16[768,3072]{1,0:T(8,128)(2,1)} %get-tuple-element.153.refs_2_, ...), custom_call_target="tpu_custom_call" | custom-call | flops 3623878656 | bytes 24787976 | tf_op jit(solution)/shard_map/outer_back/pallas_call | solution.py:100
  274.3 15.9 %wide_weight_grad.2 = (bf16[2,4,8,48,768]{4,3,2,1,0:T(8,128)(2,1)}, bf16[2,4,8,48,768]{4,3,2,1,0:T(8,128)(2,1)}) custom-call(s32[4]{0:T(128)} %pad_add_fusion.1.refs_0_, bf16[768,768]{1,0:T(8,128)(2,1)} %get-tuple-element.155.refs_1_, bf16[768,3072]{1,0:T(8,128)(2,1)} %get-tuple-element.154.refs_2_.refs_5_.refs_1_, ...), custom_call_target="tpu_custom_call" | custom-call | flops 7247757312 | bytes 21233680 | tf_op jit(solution)/shard_map/wide_weight_grad/pallas_call | solution.py:100
  290.8 14.9 %inner_back.2 = (f32[768,768]{1,0:T(8,128)}, bf16[768,768]{1,0:T(8,128)(2,1)}, bf16[768,768]{1,0:T(8,128)(2,1)}, f32[8,768]{1,0:T(8,128)}) custom-call(s32[2]{0:T(128)} %pad_add_fusion.refs_0_, bf16[768,3072]{1,0:T(8,128)(2,1)} %get-tuple-element.154.refs_2_.refs_5_.refs_1_, f32[768,768]{1,0:T(8,128)} %maximum_convert_fusion.1.refs_1_.refs_2_, ...), custom_call_target="tpu_custom_call" | custom-call | flops 4529848320 | bytes 35450888 | tf_op jit(solution)/shard_map/inner_back/pallas_call | solution.py:100
  305.7 4.4 sum_along.4.refs_10_
  310.6 20.8 %attend_back.4 = (bf16[768,384]{1,0:T(8,128)(2,1)}, bf16[768,384]{1,0:T(8,128)(2,1)}, bf16[768,384]{1,0:T(8,128)(2,1)}, bf16[768,384]{1,0:T(8,128)(2,1)}, bf16[768,384]{1,0:T(8,128)(2,1)}) custom-call(f32[2,384,128]{2,1,0:T(8,128)} %pad_maximum_fusion.2.refs_0_, bf16[768,768]{1,0:T(8,128)(2,1)} %get-tuple-element.144.refs_1_, ...), custom_call_target="tpu_custom_call" | custom-call | flops 18119393280 | bytes 16355328 | tf_op jit(solution)/shard_map/attend_back/pallas_call | solution.py:100
  331.4 21.1 %attend_back.5 = (bf16[768,384]{1,0:T(8,128)(2,1)}, bf16[768,384]{1,0:T(8,128)(2,1)}, bf16[768,384]{1,0:T(8,128)(2,1)}, bf16[768,384]{1,0:T(8,128)(2,1)}, bf16[768,384]{1,0:T(8,128)(2,1)}) custom-call(f32[2,384,128]{2,1,0:T(8,128)} %pad_maximum_fusion.2.refs_0_, bf16[768,768]{1,0:T(8,128)(2,1)} %get-tuple-element.144.refs_1_, ...), custom_call_target="tpu_custom_call" | custom-call | flops 18119393280 | bytes 16355328 | tf_op jit(solution)/shard_map/attend_back/pallas_call | solution.py:100
  354.8 1.7 collective-permute-done.15.refs_12_.refs_13_
  357.9 10.7 %project_back.2 = (f32[768,768]{1,0:T(8,128)}, f32[8,768]{1,0:T(8,128)}) custom-call(f32[768,768]{1,0:T(8,128)} %outer.2.refs_0_.refs_1_, f32[768,768]{1,0:T(8,128)} %get-tuple-element.158.refs_2_.refs_9_.refs_1_, f32[12,768]{1,0:T(8,128)} %squeeze.69.refs_1_.refs_3_.refs_4_.refs_2_, bf16[768,384]{1,0:T(8,128)(2,1)} %get-tuple-element.162.refs_9_.refs_3_.refs_4_, ...), custom_call_target="tpu_custom_call" | custom-call | flops 2717908992 | bytes 22474752 | tf_op jit(solution)/shard_map/project_back/pallas_call | solution.py:100
  368.7 5.2 sum_near.4.refs_15_
  373.8 11.3 %thin_weight_grad.2 = (bf16[2,4,4,48,768]{4,3,2,1,0:T(8,128)(2,1)}, bf16[2,4,4,48,768]{4,3,2,1,0:T(8,128)(2,1)}) custom-call(s32[4]{0:T(128)} %pad_add_fusion.1.refs_0_, bf16[768,768]{1,0:T(8,128)(2,1)} %get-tuple-element.174.refs_1_, bf16[768,768]{1,0:T(8,128)(2,1)} %get-tuple-element.147.refs_2_.refs_6_, bf16[768,768]{1,0:T(8,128)(2,1)} %get-tuple-element.175.refs_3_, ...), custom_call_target="tpu_custom_call" | custom-call | flops 3623878656 | bytes 14155792 | tf_op jit(solution)/shard_map/thin_weight_grad/pallas_call | solution.py:100
  385.2 10.4 %outer_back.3 = (bf16[768,768]{1,0:T(8,128)(2,1)}, bf16[768,3072]{1,0:T(8,128)(2,1)}, f32[1,3072]{1,0:T(1,128)}, f32[1,768]{1,0:T(1,128)}) custom-call(s32[2]{0:T(128)} %pad_add_fusion.refs_0_, f32[768,768]{1,0:T(8,128)} %get-tuple-element.172.refs_3_.refs_14_.refs_1_.refs_2_, bf16[768,3072]{1,0:T(8,128)(2,1)} %get-tuple-element.173.refs_2_, ...), custom_call_target="tpu_custom_call" | custom-call | flops 3623878656 | bytes 25181192 | tf_op jit(solution)/shard_map/outer_back/pallas_call | solution.py:100
  397.0 3.6 sum_along.5.refs_6_
  400.6 15.6 %wide_weight_grad.3 = (bf16[2,4,8,48,768]{4,3,2,1,0:T(8,128)(2,1)}, bf16[2,4,8,48,768]{4,3,2,1,0:T(8,128)(2,1)}) custom-call(s32[4]{0:T(128)} %pad_add_fusion.1.refs_0_, bf16[768,768]{1,0:T(8,128)(2,1)} %get-tuple-element.178.refs_1_, bf16[768,3072]{1,0:T(8,128)(2,1)} %get-tuple-element.177.refs_2_.refs_5_.refs_1_, ...), custom_call_target="tpu_custom_call" | custom-call | flops 7247757312 | bytes 21233680 | tf_op jit(solution)/shard_map/wide_weight_grad/pallas_call | solution.py:100
  419.0 15.3 %inner_back.3 = (f32[768,768]{1,0:T(8,128)}, bf16[768,768]{1,0:T(8,128)(2,1)}, bf16[768,768]{1,0:T(8,128)(2,1)}, f32[8,768]{1,0:T(8,128)}) custom-call(s32[2]{0:T(128)} %pad_add_fusion.refs_0_, bf16[768,3072]{1,0:T(8,128)(2,1)} %get-tuple-element.177.refs_2_.refs_5_.refs_1_, f32[768,768]{1,0:T(8,128)} %get-tuple-element.172.refs_3_.refs_14_.refs_1_.refs_2_, ...), custom_call_target="tpu_custom_call" | custom-call | flops 4529848320 | bytes 36237320 | tf_op jit(solution)/shard_map/inner_back/pallas_call | solution.py:100
  434.3 4.3 sum_along.6.refs_10_
  438.8 20.7 %attend_back.6 = (bf16[768,384]{1,0:T(8,128)(2,1)}, bf16[768,384]{1,0:T(8,128)(2,1)}, bf16[768,384]{1,0:T(8,128)(2,1)}, bf16[768,384]{1,0:T(8,128)(2,1)}, bf16[768,384]{1,0:T(8,128)(2,1)}) custom-call(f32[2,384,128]{2,1,0:T(8,128)} %pad_maximum_fusion.2.refs_0_, bf16[768,768]{1,0:T(8,128)(2,1)} %get-tuple-element.133.refs_1_, ...), custom_call_target="tpu_custom_call" | custom-call | flops 18119393280 | bytes 16355328 | tf_op jit(solution)/shard_map/attend_back/pallas_call | solution.py:100
  459.6 4.0 sum_near.5.refs_10_
  463.6 21.1 %attend_back.7 = (bf16[768,384]{1,0:T(8,128)(2,1)}, bf16[768,384]{1,0:T(8,128)(2,1)}, bf16[768,384]{1,0:T(8,128)(2,1)}, bf16[768,384]{1,0:T(8,128)(2,1)}, bf16[768,384]{1,0:T(8,128)(2,1)}) custom-call(f32[2,384,128]{2,1,0:T(8,128)} %pad_maximum_fusion.2.refs_0_, bf16[768,768]{1,0:T(8,128)(2,1)} %get-tuple-element.133.refs_1_, ...), custom_call_target="tpu_custom_call" | custom-call | flops 18119393280 | bytes 16355328 | tf_op jit(solution)/shard_map/attend_back/pallas_call | solution.py:100
  489.7 11.0 %thin_weight_grad.3 = (bf16[2,4,4,48,768]{4,3,2,1,0:T(8,128)(2,1)}, bf16[2,4,4,48,768]{4,3,2,1,0:T(8,128)(2,1)}) custom-call(s32[4]{0:T(128)} %pad_add_fusion.1.refs_0_, bf16[768,768]{1,0:T(8,128)(2,1)} %get-tuple-element.196.refs_1_, bf16[768,768]{1,0:T(8,128)(2,1)} %get-tuple-element.136.refs_2_.refs_6_, bf16[768,768]{1,0:T(8,128)(2,1)} %get-tuple-element.197.refs_3_, ...), custom_call_target="tpu_custom_call" | custom-call | flops 3623878656 | bytes 14155792 | tf_op jit(solution)/shard_map/thin_weight_grad/pallas_call | solution.py:100
  500.7 2.0 collective-permute-done.25.refs_4_
  504.3 5.2 sum_near.6.refs_5_
  511.2 4.2 adam.6
  515.4 3.9 collective-permute-done.27.refs_3_.refs_4_
  520.8 3.6 sum_along.7.refs_14_
  524.4 1.8 collective-permute-start.28
  526.2 10.8 %project_back.3 = (f32[768,768]{1,0:T(8,128)}, f32[8,768]{1,0:T(8,128)}) custom-call(f32[768,768]{1,0:T(8,128)} %maximum_convert_fusion.refs_0_.refs_1_, f32[768,768]{1,0:T(8,128)} %get-tuple-element.182.refs_2_.refs_9_.refs_1_, f32[12,768]{1,0:T(8,128)} %squeeze.68.refs_1_.refs_3_.refs_4_.refs_2_, ...), custom_call_target="tpu_custom_call" | custom-call | flops 2717908992 | bytes 22867968 | tf_op jit(solution)/shard_map/project_back/pallas_call | solution.py:100
  537.0 10.3 %outer.3.refs_5_.refs_1_ = f32[768,768]{1,0:T(8,128)} custom-call(s32[2]{0:T(128)} %pad_add_fusion.refs_0_, f32[768,768]{1,0:T(8,128)} %get-tuple-element.150.refs_3_.refs_1_, bf16[768,3072]{1,0:T(8,128)(2,1)} %get-tuple-element.151.refs_3_.refs_2_, f32[12,768]{1,0:T(8,128)} %squeeze.69.refs_1_.refs_3_.refs_4_.refs_2_, bf16[16,384,768]{2,1,0:T(8,128)(2,1)} %bitcast.79, ...), custom_call_target="tpu_custom_call" | custom-call | flops 3623878656 | bytes 21270536 | tf_op jit(solution)/shard_map/outer/pallas_call | solution.py:100
  547.3 4.0 adam.7
  553.3 4.0 sum_near.7.refs_2_.refs_5_
  557.4 2.6 small_cut.1
  562.4 1.8 collective-permute-start.30
  564.2 2.3 collective-permute-done.30.refs_3_
  567.2 2.9 part_clips.2
  570.0 1.7 collective-permute-start.31
  571.8 4.0 adam.8
  577.6 1.6 collective-permute-start.36
  579.2 2.8 collective-permute-start.37
  582.0 3.1 part_clips.3
  591.2 4.0 adam.9
  596.1 2.1 collective-permute-done.32
  599.9 3.9 adam.10
  604.6 4.0 adam.11
  (191 shorter events, 62.4 us)
Async XLA Ops:
  7.2 94.6 %all-gather.7.cloned.1.call-start = ((), (), s32[]{:S(2)}) async-start(), calls=%async_computation.9 | async-start | bytes 10444800 | tf_op jit(solution)/shard_map/all_gather | solution.py:1093
  11.7 177.8 %all-gather.5.cloned.1.call-start = ((), (), s32[]{:S(2)}) async-start(), calls=%async_computation.8 | async-start | bytes 10027008 | tf_op jit(solution)/shard_map/all_gather | solution.py:1093
  11.7 2.6 copy-start.9
  11.8 2.6 copy-start.10
  14.3 471.6 %reduce-scatter.5.cloned.1.call-start = ((), (), s32[]{:S(2)}) async-start(), calls=%async_computation.4 | async-start | bytes 2949120 | tf_op jit(solution)/shard_map/reduce_scatter | solution.py:1144
  15.5 35.7 %collective-permute-start = (bf16[2,384,768]{2,1,0:T(8,128)(2,1)}, bf16[2,384,768]{2,1,0:T(8,128)(2,1)S(1)}, u32[]{:S(2)}, u32[]{:S(2)}) collective-permute-start(bf16[2,384,768]{2,1,0:T(8,128)(2,1)} %fusion.3), channel_id=1, source_target_pairs={{0,2},{1,3},{2,0},{3,1},{4,6},{5,7},{6,4},{7,5},{8,10},{9,11},{10,... | collective-permute-start | bytes 3538952 | tf_op jit(solution)/shard_map/ppermute | solution.py:1058
  107.7 8.6 %copy-start.36 = (s32[2]{0:T(128)S(1)}, s32[2]{0:T(128)}, u32[]{:S(2)}) copy-start(s32[2]{0:T(128)} %param.13) | copy-start | bytes 28
  116.0 2.6 copy-start.6
  116.0 4.9 collective-permute-start.3
  118.6 28.1 %collective-permute-start.2 = (bf16[8,96,768]{2,1,0:T(8,128)(2,1)S(1)}, bf16[8,96,768]{2,1,0:T(8,128)(2,1)S(1)}, u32[]{:S(2)}, u32[]{:S(2)}) collective-permute-start(bf16[8,96,768]{2,1,0:T(8,128)(2,1)S(1)} %copy-done.6), channel_id=1, source_target_pairs={{0,16},{16,0},{1,17},{17,1},{2,18},{18,2},{3,19},{19,3},{4,20},{20... | collective-permute-start | bytes 3538952 | tf_op jit(solution)/shard_map/ppermute | solution.py:1108
  120.9 25.8 %copy-start.5 = (bf16[8,96,768]{2,1,0:T(8,128)(2,1)S(1)}, bf16[8,96,768]{2,1,0:T(8,128)(2,1)}, u32[]{:S(2)}) copy-start(bf16[8,96,768]{2,1,0:T(8,128)(2,1)} %get-tuple-element.266.refs_4_) | copy-start | bytes 3538948
  146.7 3.0 copy-start.14
  146.7 3.0 collective-permute-start.4
  146.7 28.4 %collective-permute-start.1 = (bf16[8,96,768]{2,1,0:T(8,128)(2,1)S(1)}, bf16[8,96,768]{2,1,0:T(8,128)(2,1)S(1)}, u32[]{:S(2)}, u32[]{:S(2)}) collective-permute-start(bf16[8,96,768]{2,1,0:T(8,128)(2,1)S(1)} %copy-done.5), channel_id=1, source_target_pairs={{0,16},{16,0},{1,17},{17,1},{2,18},{18,2},{3,19},{19,3},{4,20},{20... | collective-permute-start | bytes 3538952 | tf_op jit(solution)/shard_map/ppermute | solution.py:1108
  175.1 3.0 copy-start.12
  175.1 3.0 collective-permute-start.5
  192.7 8.8 %copy-start.8 = (bf16[8,96,768]{2,1,0:T(8,128)(2,1)S(1)}, bf16[8,96,768]{2,1,0:T(8,128)(2,1)}, u32[]{:S(2)}) copy-start(bf16[8,96,768]{2,1,0:T(8,128)(2,1)} %get-tuple-element.267.refs_3_) | copy-start | bytes 3538948
  201.5 4.7 collective-permute-start.8
  201.5 29.7 %collective-permute-start.7 = (bf16[8,96,768]{2,1,0:T(8,128)(2,1)S(1)}, bf16[8,96,768]{2,1,0:T(8,128)(2,1)S(1)}, u32[]{:S(2)}, u32[]{:S(2)}) collective-permute-start(bf16[8,96,768]{2,1,0:T(8,128)(2,1)S(1)} %copy-done.8), channel_id=1, source_target_pairs={{0,16},{16,0},{1,17},{17,1},{2,18},{18,2},{3,19},{19,3},{4,20},{20... | collective-permute-start | bytes 3538952 | tf_op jit(solution)/shard_map/ppermute | solution.py:1108
  207.7 23.7 %copy-start.7 = (bf16[8,96,768]{2,1,0:T(8,128)(2,1)S(1)}, bf16[8,96,768]{2,1,0:T(8,128)(2,1)}, u32[]{:S(2)}) copy-start(bf16[8,96,768]{2,1,0:T(8,128)(2,1)} %get-tuple-element.268.refs_4_) | copy-start | bytes 3538948
  231.2 2.9 copy-start.3
  231.2 2.9 collective-permute-start.9
  231.4 28.3 %collective-permute-start.6 = (bf16[8,96,768]{2,1,0:T(8,128)(2,1)S(1)}, bf16[8,96,768]{2,1,0:T(8,128)(2,1)}, u32[]{:S(2)}, u32[]{:S(2)}) collective-permute-start(bf16[8,96,768]{2,1,0:T(8,128)(2,1)S(1)} %copy-done.7), channel_id=1, source_target_pairs={{0,16},{16,0},{1,17},{17,1},{2,18},{18,2},{3,19},{19,3},{4,20},{20... | collective-permute-start | bytes 3538952 | tf_op jit(solution)/shard_map/ppermute | solution.py:1108
  259.7 3.3 collective-permute-start.10
  290.3 15.4 %collective-permute-start.11 = (bf16[2,4,8,48,768]{4,3,2,1,0:T(8,128)(2,1)}, bf16[2,4,8,48,768]{4,3,2,1,0:T(8,128)(2,1)}, u32[]{:S(2)}, u32[]{:S(2)}) collective-permute-start(bf16[2,4,8,48,768]{4,3,2,1,0:T(8,128)(2,1)} %get-tuple-element.161), channel_id=1, source_target_pairs={{0,1},{1,0},{2,3},{3,2},{4,5},{5,4},{6,7},{7,6},{8,9},{9,8},{10,11... | collective-permute-start | bytes 14155784 | tf_op jit(solution)/shard_map/ppermute | solution.py:1128
  310.0 58.6 %collective-permute-start.16 = (bf16[4,8,48,768]{3,2,1,0:T(8,128)(2,1)}, bf16[4,8,48,768]{3,2,1,0:T(8,128)(2,1)}, u32[]{:S(2)}, u32[]{:S(2)}) collective-permute-start(bf16[4,8,48,768]{3,2,1,0:T(8,128)(2,1)} %sum_along.4.refs_10_), channel_id=1, source_target_pairs={{0,2},{1,3},{2,0},{3,1},{4,6},{5,7},{6,4},{7,5},{8,10},{9,11},{10,... | collective-permute-start | bytes 7077896 | tf_op jit(solution)/shard_map/ppermute | solution.py:1136
  331.4 21.8 %copy-start.35 = (bf16[768,384]{1,0:T(8,128)(2,1)S(1)}, bf16[768,384]{1,0:T(8,128)(2,1)}, u32[]{:S(2)}) copy-start(bf16[768,384]{1,0:T(8,128)(2,1)} %get-tuple-element.166) | copy-start | bytes 1769476
  331.4 21.8 %copy-start.34 = (bf16[768,384]{1,0:T(8,128)(2,1)S(1)}, bf16[768,384]{1,0:T(8,128)(2,1)}, u32[]{:S(2)}) copy-start(bf16[768,384]{1,0:T(8,128)(2,1)} %get-tuple-element.170) | copy-start | bytes 1769476
  352.5 2.3 collective-permute-start.13
  352.6 3.9 collective-permute-start.15
  353.1 3.4 collective-permute-start.12
  353.2 3.9 collective-permute-start.14
  385.1 10.5 %collective-permute-start.17 = (bf16[2,4,4,48,768]{4,3,2,1,0:T(8,128)(2,1)}, bf16[2,4,4,48,768]{4,3,2,1,0:T(8,128)(2,1)S(1)}, u32[]{:S(2)}, u32[]{:S(2)}) collective-permute-start(bf16[2,4,4,48,768]{4,3,2,1,0:T(8,128)(2,1)} %get-tuple-element.180), channel_id=1, source_target_pairs={{0,1},{1,0},{2,3},{3,2},{4,5},{5,4},{6,7},{7,6},{8,9},{9,8},{10,11... | collective-permute-start | bytes 7077896 | tf_op jit(solution)/shard_map/ppermute | solution.py:1128
  416.2 18.0 %collective-permute-start.18 = (bf16[2,4,8,48,768]{4,3,2,1,0:T(8,128)(2,1)}, bf16[2,4,8,48,768]{4,3,2,1,0:T(8,128)(2,1)}, u32[]{:S(2)}, u32[]{:S(2)}) collective-permute-start(bf16[2,4,8,48,768]{4,3,2,1,0:T(8,128)(2,1)} %get-tuple-element.185), channel_id=1, source_target_pairs={{0,1},{1,0},{2,3},{3,2},{4,5},{5,4},{6,7},{7,6},{8,9},{9,8},{10,11... | collective-permute-start | bytes 14155784 | tf_op jit(solution)/shard_map/ppermute | solution.py:1128
  416.6 93.0 %reduce-scatter.7.cloned.1.call-start = ((), (), s32[]{:S(2)}) async-start(), calls=%async_computation.5 | async-start | bytes 1474560 | tf_op jit(solution)/shard_map/reduce_scatter | solution.py:1144
  417.5 42.1 %collective-permute-start.19 = (bf16[4,4,48,768]{3,2,1,0:T(8,128)(2,1)S(1)}, bf16[4,4,48,768]{3,2,1,0:T(8,128)(2,1)}, u32[]{:S(2)}, u32[]{:S(2)}) collective-permute-start(bf16[4,4,48,768]{3,2,1,0:T(8,128)(2,1)S(1)} %copy-done.23), channel_id=1, source_target_pairs={{0,2},{1,3},{2,0},{3,1},{4,6},{5,7},{6,4},{7,5},{8,10},{9,11},{10,... | collective-permute-start | bytes 3538952 | tf_op jit(solution)/shard_map/ppermute | solution.py:1136
  438.6 64.1 %collective-permute-start.26 = (bf16[4,8,48,768]{3,2,1,0:T(8,128)(2,1)}, bf16[4,8,48,768]{3,2,1,0:T(8,128)(2,1)S(1)}, u32[]{:S(2)}, u32[]{:S(2)}) collective-permute-start(bf16[4,8,48,768]{3,2,1,0:T(8,128)(2,1)} %sum_along.6.refs_10_), channel_id=1, source_target_pairs={{0,2},{1,3},{2,0},{3,1},{4,6},{5,7},{6,4},{7,5},{8,10},{9,11},{10,... | collective-permute-start | bytes 7077896 | tf_op jit(solution)/shard_map/ppermute | solution.py:1136
  463.6 112.2 %reduce-scatter.9.cloned.1.call-start = ((), (), s32[]{:S(2)}) async-start(), calls=%async_computation.6 | async-start | bytes 2949120 | tf_op jit(solution)/shard_map/reduce_scatter | solution.py:1144
  484.8 2.3 collective-permute-start.21
  484.9 3.7 collective-permute-start.23
  485.4 3.5 collective-permute-start.20
  485.4 4.3 collective-permute-start.22
  487.1 2.6 copy-start.25
  487.1 15.6 %collective-permute-start.25 = (bf16[8,48,768]{2,1,0:T(8,128)(2,1)}, bf16[8,48,768]{2,1,0:T(8,128)(2,1)S(1)}, u32[]{:S(2)}, u32[]{:S(2)}) collective-permute-start(bf16[8,48,768]{2,1,0:T(8,128)(2,1)} %bitcast.87), channel_id=1, source_target_pairs={{0,16},{16,0},{1,17},{17,1},{2,18},{18,2},{3,19},{19,3},{4,20},{20... | collective-permute-start | bytes 1769480 | tf_op jit(solution)/shard_map/ppermute | solution.py:1162
  509.5 79.5 %reduce-scatter.11.cloned.1.call-start = ((), (), s32[]{:S(2)}) async-start(), calls=%async_computation.7 | async-start | bytes 1474560 | tf_op jit(solution)/shard_map/reduce_scatter | solution.py:1144
  509.5 9.7 %collective-permute-start.24 = (bf16[2,4,4,48,768]{4,3,2,1,0:T(8,128)(2,1)}, bf16[2,4,4,48,768]{4,3,2,1,0:T(8,128)(2,1)S(1)}, u32[]{:S(2)}, u32[]{:S(2)}) collective-permute-start(bf16[2,4,4,48,768]{4,3,2,1,0:T(8,128)(2,1)} %get-tuple-element.199), channel_id=1, source_target_pairs={{0,1},{1,0},{2,3},{3,2},{4,5},{5,4},{6,7},{7,6},{8,9},{9,8},{10,11... | collective-permute-start | bytes 7077896 | tf_op jit(solution)/shard_map/ppermute | solution.py:1128
  509.7 9.6 %collective-permute-start.27 = (bf16[4,48,768]{2,1,0:T(8,128)(2,1)}, bf16[4,48,768]{2,1,0:T(8,128)(2,1)S(1)}, u32[]{:S(2)}, u32[]{:S(2)}) collective-permute-start(bf16[4,48,768]{2,1,0:T(8,128)(2,1)} %bitcast.96), channel_id=1, source_target_pairs={{0,16},{16,0},{1,17},{17,1},{2,18},{18,2},{3,19},{19,3},{4,20},{20... | collective-permute-start | bytes 884744 | tf_op jit(solution)/shard_map/ppermute | solution.py:1162
  524.4 27.9 %collective-permute-start.28 = (bf16[4,4,48,768]{3,2,1,0:T(8,128)(2,1)}, bf16[4,4,48,768]{3,2,1,0:T(8,128)(2,1)S(1)}, u32[]{:S(2)}, u32[]{:S(2)}) collective-permute-start(bf16[4,4,48,768]{3,2,1,0:T(8,128)(2,1)} %sum_along.7.refs_14_), channel_id=1, source_target_pairs={{0,2},{1,3},{2,0},{3,1},{4,6},{5,7},{6,4},{7,5},{8,10},{9,11},{10,... | collective-permute-start | bytes 3538952 | tf_op jit(solution)/shard_map/ppermute | solution.py:1136
  559.9 1.5 collective-permute-start.29
  562.4 4.2 collective-permute-start.30
  570.0 15.1 %collective-permute-start.31 = (bf16[384,768]{1,0:T(8,128)(2,1)}, bf16[384,768]{1,0:T(8,128)(2,1)S(1)}, u32[]{:S(2)}, u32[]{:S(2)}) collective-permute-start(bf16[384,768]{1,0:T(8,128)(2,1)} %get-tuple-element.214), channel_id=1, source_target_pairs={{0,2},{1,3},{2,0},{3,1},{4,6},{5,7},{6,4},{7,5},{8,10},{9,11},{10,... | collective-permute-start | bytes 1769480 | tf_op jit(solution)/shard_map/ppermute | solution.py:1070
  571.8 5.2 copy-start.29
  575.8 14.2 %collective-permute-start.34 = (bf16[8,48,768]{2,1,0:T(8,128)(2,1)}, bf16[8,48,768]{2,1,0:T(8,128)(2,1)S(1)}, u32[]{:S(2)}, u32[]{:S(2)}) collective-permute-start(bf16[8,48,768]{2,1,0:T(8,128)(2,1)} %bitcast.84), channel_id=1, source_target_pairs={{0,16},{16,0},{1,17},{17,1},{2,18},{18,2},{3,19},{19,3},{4,20},{20... | collective-permute-start | bytes 1769480 | tf_op jit(solution)/shard_map/ppermute | solution.py:1162
  577.0 18.1 %collective-permute-start.35 = (f32[24,128]{1,0:T(8,128)S(1)}, f32[24,128]{1,0:T(8,128)S(1)}, u32[]{:S(2)}, u32[]{:S(2)}) collective-permute-start(f32[24,128]{1,0:T(8,128)S(1)} %get-tuple-element.283), channel_id=1, source_target_pairs={{0,4},{4,8},{8,12},{12,0},{1,5},{5,9},{9,13},{13,1},{2,6},{6,10},{... | collective-permute-start | bytes 36872 | tf_op jit(solution)/shard_map/ppermute | solution.py:1386
  577.6 17.5 %collective-permute-start.36 = (f32[24,128]{1,0:T(8,128)S(1)}, f32[24,128]{1,0:T(8,128)S(1)}, u32[]{:S(2)}, u32[]{:S(2)}) collective-permute-start(f32[24,128]{1,0:T(8,128)S(1)} %get-tuple-element.282), channel_id=1, source_target_pairs={{0,8},{4,12},{8,0},{12,4},{1,9},{5,13},{9,1},{13,5},{2,10},{6,14},... | collective-permute-start | bytes 36872 | tf_op jit(solution)/shard_map/ppermute | solution.py:1386
  579.2 7.0 %copy-start.26 = (bf16[384,768]{1,0:T(8,128)(2,1)S(1)}, bf16[384,768]{1,0:T(8,128)(2,1)}, u32[]{:S(2)}) copy-start(bf16[384,768]{1,0:T(8,128)(2,1)} %get-tuple-element.213) | copy-start | bytes 1769476
  579.2 16.0 %collective-permute-start.37 = (f32[24,128]{1,0:T(8,128)S(1)}, f32[24,128]{1,0:T(8,128)S(1)}, u32[]{:S(2)}, u32[]{:S(2)}) collective-permute-start(f32[24,128]{1,0:T(8,128)S(1)} %get-tuple-element.281), channel_id=1, source_target_pairs={{0,12},{4,0},{8,4},{12,8},{1,13},{5,1},{9,5},{13,9},{2,14},{6,2},{... | collective-permute-start | bytes 36872 | tf_op jit(solution)/shard_map/ppermute | solution.py:1386
  585.1 13.1 %collective-permute-start.32 = (bf16[384,768]{1,0:T(8,128)(2,1)}, bf16[384,768]{1,0:T(8,128)(2,1)S(1)}, u32[]{:S(2)}, u32[]{:S(2)}) collective-permute-start(bf16[384,768]{1,0:T(8,128)(2,1)} %get-tuple-element.224), channel_id=1, source_target_pairs={{0,2},{1,3},{2,0},{3,1},{4,6},{5,7},{6,4},{7,5},{8,10},{9,11},{10,... | collective-permute-start | bytes 1769480 | tf_op jit(solution)/shard_map/ppermute | solution.py:1070
  590.0 8.2 %copy-start.22 = (f32[384,768]{1,0:T(8,128)S(1)}, f32[384,768]{1,0:T(8,128)}, u32[]{:S(2)}) copy-start(f32[384,768]{1,0:T(8,128)} %get-tuple-element.223) | copy-start | bytes 3538948
  590.0 13.9 %collective-permute-start.33 = (bf16[4,48,768]{2,1,0:T(8,128)(2,1)}, bf16[4,48,768]{2,1,0:T(8,128)(2,1)S(1)}, u32[]{:S(2)}, u32[]{:S(2)}) collective-permute-start(bf16[4,48,768]{2,1,0:T(8,128)(2,1)} %bitcast.91), channel_id=1, source_target_pairs={{0,16},{16,0},{1,17},{17,1},{2,18},{18,2},{3,19},{19,3},{4,20},{20... | collective-permute-start | bytes 884744 | tf_op jit(solution)/shard_map/ppermute | solution.py:1162
  595.2 13.4 %collective-permute-start.38 = (bf16[2,12,48]{2,1,0:T(8,128)(2,1)S(1)}, bf16[2,12,48]{2,1,0:T(8,128)(2,1)S(1)}, u32[]{:S(2)}, u32[]{:S(2)}) collective-permute-start(bf16[2,12,48]{2,1,0:T(8,128)(2,1)S(1)} %convert_element_type.43), channel_id=1, source_target_pairs={{0,16},{16,0},{1,17},{17,1},{2,18},{18,2},{3,19},{19,3},{4,20},{20... | collective-permute-start | bytes 6920 | tf_op jit(solution)/shard_map/ppermute | solution.py:1421
  604.6 4.0 copy-start.30
  604.6 4.0 copy-start.31
  604.6 4.0 copy-start.32
  (18 other events, 20.4 us)
Sparse Core Ops, SparseCore 0:
  11.8 89.9 all-gather.6
  104.6 79.6 all-gather.4
  416.8 47.6 reduce-scatter.4
  467.2 28.6 reduce-scatter.6
  509.6 47.6 reduce-scatter.8
  559.5 29.4 reduce-scatter.10
where the time goes:
time: 630 us; the launch traced here: 618 us
  Pallas kernels  397 us (63%)
  waiting for transfers between devices  131 us (21%)
  starting transfers between devices  33.2 us (5%)
  local copies, waits for them, and re-layouts  29 us (5%)
  between operations  15 us (2%)
  other arithmetic  12.8 us (2%)
    pallas_call x41, Pallas kernels, run(): pl.pallas_call(body, grid_spec=grid_spec, out_shape=list(out_shapes), inp...  397 us
    all_gather x2, waiting for transfers between devices, gather(): chunk = lax.all_gather(own, ('fsdp', 'seq'), axis=0)  47.9 us
    ppermute x1, waiting for transfers between devices, to_clips(): taken = lax.ppermute(given, 'seq', swap)  32.8 us
    ppermute x4, waiting for transfers between devices, share(): lax.ppermute(part, 'rep', turn('rep', 1))  21.2 us
    unnamed x79, local copies, waits for them, and re-layouts  15.6 us
  transfers between devices with their start and end apart: 45, of which 24 were waited for; matrix products, arithmetic and copies ran while one was open for 3% of the time, Pallas kernels for 52%

commit v1 on v0

--- a/solution.py
+++ b/solution.py
@@ -1205,12 +1205,12 @@
     for layer_index in range(layer_count):
         params = params_all[layer_index]
         wide = wides[layer_index]
-        hidden = share(wide, hidden)
         normed_low, queries, own = project(
-            hidden, params, wide.chunk, wide.block, wide.thin_at, wide.given
+            hidden, params, wide.chunk, wide.block, wide.thin_at, []
         )
+        own = share(wide, own)
         others = [lax.ppermute(own, "seq", around(step)) for step in range(1, half)]
-        mixed_out, log_total = attend(queries, own, others, bias, [])
+        mixed_out, log_total = attend(queries, own, others, bias, wide.given)
         mixed_out = exchange(wide, 0, mixed_out)
         middle, second_low, active, slope = inner(hidden, mixed_out, params, wide, [])
         middle = exchange(wide, 1, middle)

time: 630 us -> 628 us (level)
    unnamed x79 -> x81, local copies, waits for them, and re-layouts: 15.6 us -> 15.3 us
  transfers between devices with their start and end apart: 45 -> 45, of which waited for: 24 -> 25; matrix products, arithmetic and copies ran while one was open for 3% -> 4% of each run, Pallas kernels for 52% -> 52%
where the time goes in v1:
time: 628 us; the launch traced here: 616 us
  Pallas kernels  397 us (63%)
  waiting for transfers between devices  132 us (21%)
  starting transfers between devices  32.7 us (5%)
  local copies, waits for them, and re-layouts  27.1 us (4%)
  between operations  15 us (2%)
  other arithmetic  12.8 us (2%)
    pallas_call x41, Pallas kernels, run(): pl.pallas_call(body, grid_spec=grid_spec, out_shape=list(out_shapes), inp...  397 us
    all_gather x2, waiting for transfers between devices, gather(): chunk = lax.all_gather(own, ('fsdp', 'seq'), axis=0)  47.7 us
    ppermute x1, waiting for transfers between devices, to_clips(): taken = lax.ppermute(given, 'seq', swap)  32.8 us
    ppermute x4, waiting for transfers between devices, share(): lax.ppermute(part, 'rep', turn('rep', 1))  24.4 us
    unnamed x81, local copies, waits for them, and re-layouts  15.3 us
  transfers between devices with their start and end apart: 45, of which 25 were waited for; matrix products, arithmetic and copies ran while one was open for 4% of the time, Pallas kernels for 52%

profile of v1, /device:TPU:0, one launch (start us, length us, event | category | flops | bytes accessed | tf_op | source)
XLA Modules:
  0.0 616.3 jit_solution(7349524714306929293)
XLA Ops:
  9.3 2.4 pack.3
  11.8 2.5 pack.2
  15.5 3.0 collective-permute-start
  18.5 32.8 %collective-permute-done = bf16[2,384,768]{2,1,0:T(8,128)(2,1)S(1)} collective-permute-done((bf16[2,384,768]{2,1,0:T(8,128)(2,1)}, bf16[2,384,768]{2,1,0:T(8,128)(2,1)S(1)}, u32[]{:S(2)}, u32[]{:S(2)}) %collective-permute-start) | collective-permute-done | bytes 1179680 | tf_op jit(solution)/shard_map/ppermute | solution.py:1058
  52.6 1.6 maximum_convert_fusion.refs_0_.refs_1_
  54.1 47.7 %all-gather.7.cloned.1.call-done = bf16[6400,768]{1,0:T(8,128)(2,1)} async-done(((bf16[400,768]{1,0:T(8,128)(2,1)}), bf16[6400,768]{1,0:T(8,128)(2,1)}) %all-gather.7.cloned.1.call-update) | async-done | bytes 9830416 | tf_op jit(solution)/shard_map/all_gather | solution.py:1093
  104.6 8.3 %project.2 = (bf16[768,768]{1,0:T(8,128)(2,1)}, bf16[768,768]{1,0:T(8,128)(2,1)}, bf16[768,1536]{1,0:T(8,128)(2,1)}) custom-call(f32[768,768]{1,0:T(8,128)} %maximum_convert_fusion.refs_0_.refs_1_, f32[12,768]{1,0:T(8,128)} %squeeze.67.refs_1_.refs_3_.refs_4_.refs_2_, bf16[16,400,768]{2,1,0:T(8,128)(2,1)} %bitcast.62), custom_call_target="tpu_custom_call" | custom-call | flops 2717908992 | bytes 16945152 | tf_op jit(solution)/shard_map/project/pallas_call | solution.py:100
  115.4 2.8 constant_dynamic-slice_fusion.2
  119.6 23.4 %attend.2 = (bf16[768,768]{1,0:T(8,128)(2,1)}, f32[6,2,768]{2,1,0:T(2,128)}) custom-call(f32[2,384,128]{2,1,0:T(8,128)} %pad_maximum_fusion.2.refs_0_, bf16[768,768]{1,0:T(8,128)(2,1)} %get-tuple-element.133.refs_1_, bf16[768,1536]{1,0:T(8,128)(2,1)} %get-tuple-element.134.refs_2_.refs_4_, bf16[768,1536]{1,0:T(8,128)(2,1)} %collective-permute-done.3.refs_3_.refs_5_, ...), custom_call_target="tpu_custom_call" | custom-call | flops 14495514624 | bytes 12226560 | tf_op jit(solution)/shard_map/attend/pallas_call | solution.py:100
  143.0 3.3 collective-permute-done.2.refs_6_.refs_7_
  150.2 15.5 %inner.2 = (f32[768,768]{1,0:T(8,128)}, bf16[768,768]{1,0:T(8,128)(2,1)}, bf16[768,3072]{1,0:T(8,128)(2,1)}, bf16[768,3072]{1,0:T(8,128)(2,1)}) custom-call(s32[2]{0:T(128)} %pad_add_fusion.refs_0_, f32[768,768]{1,0:T(8,128)} %maximum_convert_fusion.refs_0_.refs_1_, bf16[768,768]{1,0:T(8,128)(2,1)} %get-tuple-element.136.refs_2_.refs_6_, ...), custom_call_target="tpu_custom_call" | custom-call | flops 4529848320 | bytes 38572040 | tf_op jit(solution)/shard_map/inner/pallas_call | solution.py:100
  165.7 9.2 %collective-permute-done.1.refs_5_.refs_4_ = bf16[8,96,768]{2,1,0:T(8,128)(2,1)S(1)} collective-permute-done((bf16[8,96,768]{2,1,0:T(8,128)(2,1)}, bf16[8,96,768]{2,1,0:T(8,128)(2,1)S(1)}, u32[]{:S(2)}, u32[]{:S(2)}) %collective-permute-start.1) | collective-permute-done | bytes 1179680 | tf_op jit(solution)/shard_map/ppermute | solution.py:1108
  175.8 2.3 collective-permute-done.5.refs_6_.refs_5_
  179.1 10.4 %outer.2.refs_0_.refs_1_ = f32[768,768]{1,0:T(8,128)} custom-call(s32[2]{0:T(128)} %pad_add_fusion.refs_0_, f32[768,768]{1,0:T(8,128)} %get-tuple-element.139.refs_1_.refs_3_, bf16[768,3072]{1,0:T(8,128)(2,1)} %get-tuple-element.140.refs_2_.refs_3_, f32[12,768]{1,0:T(8,128)} %squeeze.67.refs_1_.refs_3_.refs_4_.refs_2_, bf16[16,400,768]{2,1,0:T(8,128)(2,1)} %bitcast.66, ...), custom_call_target="tpu_custom_call" | custom-call | flops 3623878656 | bytes 21663752 | tf_op jit(solution)/shard_map/outer/pallas_call | solution.py:100
  189.5 8.7 %project.3 = (bf16[768,768]{1,0:T(8,128)(2,1)}, bf16[768,768]{1,0:T(8,128)(2,1)}, bf16[768,1536]{1,0:T(8,128)(2,1)}) custom-call(f32[768,768]{1,0:T(8,128)} %outer.2.refs_0_.refs_1_, f32[12,768]{1,0:T(8,128)} %squeeze.69.refs_1_.refs_3_.refs_4_.refs_2_, bf16[16,384,768]{2,1,0:T(8,128)(2,1)} %bitcast.71), custom_call_target="tpu_custom_call" | custom-call | flops 2717908992 | bytes 16551936 | tf_op jit(solution)/shard_map/project/pallas_call | solution.py:100
  198.3 2.8 constant_dynamic-slice_fusion
  203.1 23.4 %attend.3 = (bf16[768,768]{1,0:T(8,128)(2,1)}, f32[6,2,768]{2,1,0:T(2,128)}) custom-call(f32[2,384,128]{2,1,0:T(8,128)} %pad_maximum_fusion.2.refs_0_, bf16[768,768]{1,0:T(8,128)(2,1)} %get-tuple-element.144.refs_1_, bf16[768,1536]{1,0:T(8,128)(2,1)} %get-tuple-element.145.refs_2_.refs_4_, bf16[768,1536]{1,0:T(8,128)(2,1)} %collective-permute-done.8.refs_3_.refs_5_, ...), custom_call_target="tpu_custom_call" | custom-call | flops 14495514624 | bytes 12226560 | tf_op jit(solution)/shard_map/attend/pallas_call | solution.py:100
  226.6 2.8 collective-permute-done.7.refs_6_.refs_7_
  233.3 15.5 %inner.3 = (f32[768,768]{1,0:T(8,128)}, bf16[768,768]{1,0:T(8,128)(2,1)}, bf16[768,3072]{1,0:T(8,128)(2,1)}, bf16[768,3072]{1,0:T(8,128)(2,1)}) custom-call(s32[2]{0:T(128)} %pad_add_fusion.refs_0_, f32[768,768]{1,0:T(8,128)} %outer.2.refs_0_.refs_1_, bf16[768,768]{1,0:T(8,128)(2,1)} %get-tuple-element.147.refs_2_.refs_6_, ...), custom_call_target="tpu_custom_call" | custom-call | flops 4529848320 | bytes 37785608 | tf_op jit(solution)/shard_map/inner/pallas_call | solution.py:100
  248.9 9.1 %collective-permute-done.6.refs_4_.refs_5_ = bf16[8,96,768]{2,1,0:T(8,128)(2,1)S(1)} collective-permute-done((bf16[8,96,768]{2,1,0:T(8,128)(2,1)}, bf16[8,96,768]{2,1,0:T(8,128)(2,1)S(1)}, u32[]{:S(2)}, u32[]{:S(2)}) %collective-permute-start.6) | collective-permute-done | bytes 1179680 | tf_op jit(solution)/shard_map/ppermute | solution.py:1108
  258.7 2.7 maximum_convert_fusion.1.refs_1_.refs_2_
  262.4 10.4 %outer_back.2 = (bf16[768,768]{1,0:T(8,128)(2,1)}, bf16[768,3072]{1,0:T(8,128)(2,1)}, f32[1,3072]{1,0:T(1,128)}, f32[1,768]{1,0:T(1,128)}) custom-call(s32[2]{0:T(128)} %pad_add_fusion.refs_0_, f32[768,768]{1,0:T(8,128)} %maximum_convert_fusion.1.refs_1_.refs_2_, bf16[768,3072]{1,0:T(8,128)(2,1)} %get-tuple-element.153.refs_2_, ...), custom_call_target="tpu_custom_call" | custom-call | flops 3623878656 | bytes 24787976 | tf_op jit(solution)/shard_map/outer_back/pallas_call | solution.py:100
  272.8 15.8 %wide_weight_grad.2 = (bf16[2,4,8,48,768]{4,3,2,1,0:T(8,128)(2,1)}, bf16[2,4,8,48,768]{4,3,2,1,0:T(8,128)(2,1)}) custom-call(s32[4]{0:T(128)} %pad_add_fusion.1.refs_0_, bf16[768,768]{1,0:T(8,128)(2,1)} %get-tuple-element.155.refs_1_, bf16[768,3072]{1,0:T(8,128)(2,1)} %get-tuple-element.154.refs_2_.refs_5_.refs_1_, ...), custom_call_target="tpu_custom_call" | custom-call | flops 7247757312 | bytes 21233680 | tf_op jit(solution)/shard_map/wide_weight_grad/pallas_call | solution.py:100
  289.0 14.7 %inner_back.2 = (f32[768,768]{1,0:T(8,128)}, bf16[768,768]{1,0:T(8,128)(2,1)}, bf16[768,768]{1,0:T(8,128)(2,1)}, f32[8,768]{1,0:T(8,128)}) custom-call(s32[2]{0:T(128)} %pad_add_fusion.refs_0_, bf16[768,3072]{1,0:T(8,128)(2,1)} %get-tuple-element.154.refs_2_.refs_5_.refs_1_, f32[768,768]{1,0:T(8,128)} %maximum_convert_fusion.1.refs_1_.refs_2_, ...), custom_call_target="tpu_custom_call" | custom-call | flops 4529848320 | bytes 35450888 | tf_op jit(solution)/shard_map/inner_back/pallas_call | solution.py:100
  303.7 4.4 sum_along.4.refs_10_
  308.6 20.7 %attend_back.4 = (bf16[768,384]{1,0:T(8,128)(2,1)}, bf16[768,384]{1,0:T(8,128)(2,1)}, bf16[768,384]{1,0:T(8,128)(2,1)}, bf16[768,384]{1,0:T(8,128)(2,1)}, bf16[768,384]{1,0:T(8,128)(2,1)}) custom-call(f32[2,384,128]{2,1,0:T(8,128)} %pad_maximum_fusion.2.refs_0_, bf16[768,768]{1,0:T(8,128)(2,1)} %get-tuple-element.144.refs_1_, ...), custom_call_target="tpu_custom_call" | custom-call | flops 18119393280 | bytes 16355328 | tf_op jit(solution)/shard_map/attend_back/pallas_call | solution.py:100
  329.4 21.1 %attend_back.5 = (bf16[768,384]{1,0:T(8,128)(2,1)}, bf16[768,384]{1,0:T(8,128)(2,1)}, bf16[768,384]{1,0:T(8,128)(2,1)}, bf16[768,384]{1,0:T(8,128)(2,1)}, bf16[768,384]{1,0:T(8,128)(2,1)}) custom-call(f32[2,384,128]{2,1,0:T(8,128)} %pad_maximum_fusion.2.refs_0_, bf16[768,768]{1,0:T(8,128)(2,1)} %get-tuple-element.144.refs_1_, ...), custom_call_target="tpu_custom_call" | custom-call | flops 18119393280 | bytes 16355328 | tf_op jit(solution)/shard_map/attend_back/pallas_call | solution.py:100
  352.8 1.7 collective-permute-done.15.refs_12_.refs_13_
  355.9 10.7 %project_back.2 = (f32[768,768]{1,0:T(8,128)}, f32[8,768]{1,0:T(8,128)}) custom-call(f32[768,768]{1,0:T(8,128)} %outer.2.refs_0_.refs_1_, f32[768,768]{1,0:T(8,128)} %get-tuple-element.158.refs_2_.refs_9_.refs_1_, f32[12,768]{1,0:T(8,128)} %squeeze.69.refs_1_.refs_3_.refs_4_.refs_2_, bf16[768,384]{1,0:T(8,128)(2,1)} %get-tuple-element.162.refs_9_.refs_3_.refs_4_, ...), custom_call_target="tpu_custom_call" | custom-call | flops 2717908992 | bytes 22474752 | tf_op jit(solution)/shard_map/project_back/pallas_call | solution.py:100
  366.7 5.2 sum_near.4.refs_15_
  371.8 11.3 %thin_weight_grad.2 = (bf16[2,4,4,48,768]{4,3,2,1,0:T(8,128)(2,1)}, bf16[2,4,4,48,768]{4,3,2,1,0:T(8,128)(2,1)}) custom-call(s32[4]{0:T(128)} %pad_add_fusion.1.refs_0_, bf16[768,768]{1,0:T(8,128)(2,1)} %get-tuple-element.174.refs_1_, bf16[768,768]{1,0:T(8,128)(2,1)} %get-tuple-element.147.refs_2_.refs_6_, bf16[768,768]{1,0:T(8,128)(2,1)} %get-tuple-element.175.refs_3_, ...), custom_call_target="tpu_custom_call" | custom-call | flops 3623878656 | bytes 14155792 | tf_op jit(solution)/shard_map/thin_weight_grad/pallas_call | solution.py:100
  383.2 10.3 %outer_back.3 = (bf16[768,768]{1,0:T(8,128)(2,1)}, bf16[768,3072]{1,0:T(8,128)(2,1)}, f32[1,3072]{1,0:T(1,128)}, f32[1,768]{1,0:T(1,128)}) custom-call(s32[2]{0:T(128)} %pad_add_fusion.refs_0_, f32[768,768]{1,0:T(8,128)} %get-tuple-element.172.refs_3_.refs_14_.refs_1_.refs_2_, bf16[768,3072]{1,0:T(8,128)(2,1)} %get-tuple-element.173.refs_2_, ...), custom_call_target="tpu_custom_call" | custom-call | flops 3623878656 | bytes 25181192 | tf_op jit(solution)/shard_map/outer_back/pallas_call | solution.py:100
  394.9 3.6 sum_along.5.refs_6_
  398.6 15.6 %wide_weight_grad.3 = (bf16[2,4,8,48,768]{4,3,2,1,0:T(8,128)(2,1)}, bf16[2,4,8,48,768]{4,3,2,1,0:T(8,128)(2,1)}) custom-call(s32[4]{0:T(128)} %pad_add_fusion.1.refs_0_, bf16[768,768]{1,0:T(8,128)(2,1)} %get-tuple-element.178.refs_1_, bf16[768,3072]{1,0:T(8,128)(2,1)} %get-tuple-element.177.refs_2_.refs_5_.refs_1_, ...), custom_call_target="tpu_custom_call" | custom-call | flops 7247757312 | bytes 21233680 | tf_op jit(solution)/shard_map/wide_weight_grad/pallas_call | solution.py:100
  416.9 15.4 %inner_back.3 = (f32[768,768]{1,0:T(8,128)}, bf16[768,768]{1,0:T(8,128)(2,1)}, bf16[768,768]{1,0:T(8,128)(2,1)}, f32[8,768]{1,0:T(8,128)}) custom-call(s32[2]{0:T(128)} %pad_add_fusion.refs_0_, bf16[768,3072]{1,0:T(8,128)(2,1)} %get-tuple-element.177.refs_2_.refs_5_.refs_1_, f32[768,768]{1,0:T(8,128)} %get-tuple-element.172.refs_3_.refs_14_.refs_1_.refs_2_, ...), custom_call_target="tpu_custom_call" | custom-call | flops 4529848320 | bytes 36237320 | tf_op jit(solution)/shard_map/inner_back/pallas_call | solution.py:100
  432.3 4.3 sum_along.6.refs_10_
  436.8 20.7 %attend_back.6 = (bf16[768,384]{1,0:T(8,128)(2,1)}, bf16[768,384]{1,0:T(8,128)(2,1)}, bf16[768,384]{1,0:T(8,128)(2,1)}, bf16[768,384]{1,0:T(8,128)(2,1)}, bf16[768,384]{1,0:T(8,128)(2,1)}) custom-call(f32[2,384,128]{2,1,0:T(8,128)} %pad_maximum_fusion.2.refs_0_, bf16[768,768]{1,0:T(8,128)(2,1)} %get-tuple-element.133.refs_1_, ...), custom_call_target="tpu_custom_call" | custom-call | flops 18119393280 | bytes 16355328 | tf_op jit(solution)/shard_map/attend_back/pallas_call | solution.py:100
  457.5 4.0 sum_near.5.refs_10_
  461.6 21.1 %attend_back.7 = (bf16[768,384]{1,0:T(8,128)(2,1)}, bf16[768,384]{1,0:T(8,128)(2,1)}, bf16[768,384]{1,0:T(8,128)(2,1)}, bf16[768,384]{1,0:T(8,128)(2,1)}, bf16[768,384]{1,0:T(8,128)(2,1)}) custom-call(f32[2,384,128]{2,1,0:T(8,128)} %pad_maximum_fusion.2.refs_0_, bf16[768,768]{1,0:T(8,128)(2,1)} %get-tuple-element.133.refs_1_, ...), custom_call_target="tpu_custom_call" | custom-call | flops 18119393280 | bytes 16355328 | tf_op jit(solution)/shard_map/attend_back/pallas_call | solution.py:100
  487.6 11.0 %thin_weight_grad.3 = (bf16[2,4,4,48,768]{4,3,2,1,0:T(8,128)(2,1)}, bf16[2,4,4,48,768]{4,3,2,1,0:T(8,128)(2,1)}) custom-call(s32[4]{0:T(128)} %pad_add_fusion.1.refs_0_, bf16[768,768]{1,0:T(8,128)(2,1)} %get-tuple-element.196.refs_1_, bf16[768,768]{1,0:T(8,128)(2,1)} %get-tuple-element.136.refs_2_.refs_6_, bf16[768,768]{1,0:T(8,128)(2,1)} %get-tuple-element.197.refs_3_, ...), custom_call_target="tpu_custom_call" | custom-call | flops 3623878656 | bytes 14155792 | tf_op jit(solution)/shard_map/thin_weight_grad/pallas_call | solution.py:100
  498.6 2.0 collective-permute-done.25.refs_4_
  502.2 5.2 sum_near.6.refs_5_
  509.1 4.3 adam.6
  513.4 3.8 collective-permute-done.27.refs_3_.refs_4_
  518.7 3.6 sum_along.7.refs_14_
  522.3 1.8 collective-permute-start.28
  524.2 10.8 %project_back.3 = (f32[768,768]{1,0:T(8,128)}, f32[8,768]{1,0:T(8,128)}) custom-call(f32[768,768]{1,0:T(8,128)} %maximum_convert_fusion.refs_0_.refs_1_, f32[768,768]{1,0:T(8,128)} %get-tuple-element.182.refs_2_.refs_9_.refs_1_, f32[12,768]{1,0:T(8,128)} %squeeze.67.refs_1_.refs_3_.refs_4_.refs_2_, ...), custom_call_target="tpu_custom_call" | custom-call | flops 2717908992 | bytes 22867968 | tf_op jit(solution)/shard_map/project_back/pallas_call | solution.py:100
  534.9 10.3 %outer.3.refs_5_.refs_1_ = f32[768,768]{1,0:T(8,128)} custom-call(s32[2]{0:T(128)} %pad_add_fusion.refs_0_, f32[768,768]{1,0:T(8,128)} %get-tuple-element.150.refs_3_.refs_1_, bf16[768,3072]{1,0:T(8,128)(2,1)} %get-tuple-element.151.refs_3_.refs_2_, f32[12,768]{1,0:T(8,128)} %squeeze.69.refs_1_.refs_3_.refs_4_.refs_2_, bf16[16,384,768]{2,1,0:T(8,128)(2,1)} %bitcast.79, ...), custom_call_target="tpu_custom_call" | custom-call | flops 3623878656 | bytes 21270536 | tf_op jit(solution)/shard_map/outer/pallas_call | solution.py:100
  545.2 4.0 adam.7
  551.3 4.0 sum_near.7.refs_2_.refs_5_
  555.3 2.6 small_cut.1
  560.3 1.8 collective-permute-start.30
  562.1 2.3 collective-permute-done.30.refs_3_
  565.1 2.9 part_clips.2
  568.0 1.8 collective-permute-start.31
  569.7 4.0 adam.8
  576.5 2.6 collective-permute-start.37
  579.1 3.1 part_clips.3
  582.4 1.7 collective-permute-start.32
  585.9 2.0 collective-permute-done.34.refs_4_
  589.4 4.0 adam.9
  594.3 1.8 collective-permute-done.32
  597.8 3.9 adam.10
  602.5 4.0 adam.11
  (193 shorter events, 61.1 us)
Async XLA Ops:
  7.2 94.6 %all-gather.7.cloned.1.call-start = ((), (), s32[]{:S(2)}) async-start(), calls=%async_computation.9 | async-start | bytes 10444800 | tf_op jit(solution)/shard_map/all_gather | solution.py:1093
  11.7 177.8 %all-gather.5.cloned.1.call-start = ((), (), s32[]{:S(2)}) async-start(), calls=%async_computation.8 | async-start | bytes 10027008 | tf_op jit(solution)/shard_map/all_gather | solution.py:1093
  11.8 2.6 copy-start.5
  11.8 2.6 copy-start.6
  14.3 469.5 %reduce-scatter.5.cloned.1.call-start = ((), (), s32[]{:S(2)}) async-start(), calls=%async_computation.4 | async-start | bytes 2949120 | tf_op jit(solution)/shard_map/reduce_scatter | solution.py:1144
  15.5 35.7 %collective-permute-start = (bf16[2,384,768]{2,1,0:T(8,128)(2,1)}, bf16[2,384,768]{2,1,0:T(8,128)(2,1)S(1)}, u32[]{:S(2)}, u32[]{:S(2)}) collective-permute-start(bf16[2,384,768]{2,1,0:T(8,128)(2,1)} %fusion.3), channel_id=1, source_target_pairs={{0,2},{1,3},{2,0},{3,1},{4,6},{5,7},{6,4},{7,5},{8,10},{9,11},{10,... | collective-permute-start | bytes 3538952 | tf_op jit(solution)/shard_map/ppermute | solution.py:1058
  104.6 8.5 %copy-start.37 = (s32[2]{0:T(128)S(1)}, s32[2]{0:T(128)}, u32[]{:S(2)}) copy-start(s32[2]{0:T(128)} %param.13) | copy-start | bytes 28
  112.8 6.8 %collective-permute-start.3 = (bf16[768,1536]{1,0:T(8,128)(2,1)}, bf16[768,1536]{1,0:T(8,128)(2,1)}, u32[]{:S(2)}, u32[]{:S(2)}) collective-permute-start(bf16[768,1536]{1,0:T(8,128)(2,1)} %get-tuple-element.134.refs_2_.refs_4_), channel_id=1, source_target_pairs={{0,1},{1,0},{2,3},{3,2},{4,5},{5,4},{6,7},{7,6},{8,9},{9,8},{10,11... | collective-permute-start | bytes 7077896 | tf_op jit(solution)/shard_map/ppermute | solution.py:1212
  118.2 28.2 %collective-permute-start.2 = (bf16[8,96,768]{2,1,0:T(8,128)(2,1)S(1)}, bf16[8,96,768]{2,1,0:T(8,128)(2,1)S(1)}, u32[]{:S(2)}, u32[]{:S(2)}) collective-permute-start(bf16[8,96,768]{2,1,0:T(8,128)(2,1)S(1)} %get-tuple-element.265.refs_6_), channel_id=1, source_target_pairs={{0,16},{16,0},{1,17},{17,1},{2,18},{18,2},{3,19},{19,3},{4,20},{20... | collective-permute-start | bytes 3538952 | tf_op jit(solution)/shard_map/ppermute | solution.py:1108
  146.3 2.9 copy-start.11
  146.3 28.6 %copy-start.28 = (f32[1,12,16,48]{3,1,0,2:T(8,128)S(1)}, f32[1,12,16,48]{3,1,0,2:T(8,128)}, u32[]{:S(2)}) copy-start(f32[1,12,16,48]{3,1,0,2:T(8,128)} %get-tuple-element.279) | copy-start | bytes 110596
  146.3 2.8 collective-permute-start.4
  146.3 28.6 %collective-permute-start.1 = (bf16[8,96,768]{2,1,0:T(8,128)(2,1)}, bf16[8,96,768]{2,1,0:T(8,128)(2,1)S(1)}, u32[]{:S(2)}, u32[]{:S(2)}) collective-permute-start(bf16[8,96,768]{2,1,0:T(8,128)(2,1)} %get-tuple-element.266.refs_7_), channel_id=1, source_target_pairs={{0,16},{16,0},{1,17},{17,1},{2,18},{18,2},{3,19},{19,3},{4,20},{20... | collective-permute-start | bytes 3538952 | tf_op jit(solution)/shard_map/ppermute | solution.py:1108
  174.9 3.2 copy-start.9
  174.9 3.2 collective-permute-start.5
  198.2 4.9 collective-permute-start.8
  201.1 28.3 %collective-permute-start.7 = (bf16[8,96,768]{2,1,0:T(8,128)(2,1)S(1)}, bf16[8,96,768]{2,1,0:T(8,128)(2,1)S(1)}, u32[]{:S(2)}, u32[]{:S(2)}) collective-permute-start(bf16[8,96,768]{2,1,0:T(8,128)(2,1)S(1)} %get-tuple-element.267.refs_6_), channel_id=1, source_target_pairs={{0,16},{16,0},{1,17},{17,1},{2,18},{18,2},{3,19},{19,3},{4,20},{20... | collective-permute-start | bytes 3538952 | tf_op jit(solution)/shard_map/ppermute | solution.py:1108
  229.4 2.9 copy-start.3
  229.4 29.3 %copy-start.18 = (bf16[384,768]{1,0:T(8,128)(2,1)S(1)}, bf16[384,768]{1,0:T(8,128)(2,1)}, u32[]{:S(2)}) copy-start(bf16[384,768]{1,0:T(8,128)(2,1)} %get-tuple-element.277) | copy-start | bytes 1769476
  229.4 2.8 collective-permute-start.9
  229.4 28.6 %collective-permute-start.6 = (bf16[8,96,768]{2,1,0:T(8,128)(2,1)}, bf16[8,96,768]{2,1,0:T(8,128)(2,1)S(1)}, u32[]{:S(2)}, u32[]{:S(2)}) collective-permute-start(bf16[8,96,768]{2,1,0:T(8,128)(2,1)} %get-tuple-element.268.refs_7_), channel_id=1, source_target_pairs={{0,16},{16,0},{1,17},{17,1},{2,18},{18,2},{3,19},{19,3},{4,20},{20... | collective-permute-start | bytes 3538952 | tf_op jit(solution)/shard_map/ppermute | solution.py:1108
  258.0 3.3 copy-start.7
  258.0 3.3 collective-permute-start.10
  288.6 15.1 %collective-permute-start.11 = (bf16[2,4,8,48,768]{4,3,2,1,0:T(8,128)(2,1)}, bf16[2,4,8,48,768]{4,3,2,1,0:T(8,128)(2,1)}, u32[]{:S(2)}, u32[]{:S(2)}) collective-permute-start(bf16[2,4,8,48,768]{4,3,2,1,0:T(8,128)(2,1)} %get-tuple-element.161), channel_id=1, source_target_pairs={{0,1},{1,0},{2,3},{3,2},{4,5},{5,4},{6,7},{7,6},{8,9},{9,8},{10,11... | collective-permute-start | bytes 14155784 | tf_op jit(solution)/shard_map/ppermute | solution.py:1128
  308.1 58.6 %collective-permute-start.16 = (bf16[4,8,48,768]{3,2,1,0:T(8,128)(2,1)}, bf16[4,8,48,768]{3,2,1,0:T(8,128)(2,1)}, u32[]{:S(2)}, u32[]{:S(2)}) collective-permute-start(bf16[4,8,48,768]{3,2,1,0:T(8,128)(2,1)} %sum_along.4.refs_10_), channel_id=1, source_target_pairs={{0,2},{1,3},{2,0},{3,1},{4,6},{5,7},{6,4},{7,5},{8,10},{9,11},{10,... | collective-permute-start | bytes 7077896 | tf_op jit(solution)/shard_map/ppermute | solution.py:1136
  329.4 21.7 %copy-start.36 = (bf16[768,384]{1,0:T(8,128)(2,1)S(1)}, bf16[768,384]{1,0:T(8,128)(2,1)}, u32[]{:S(2)}) copy-start(bf16[768,384]{1,0:T(8,128)(2,1)} %get-tuple-element.166) | copy-start | bytes 1769476
  329.4 21.8 %copy-start.35 = (bf16[768,384]{1,0:T(8,128)(2,1)S(1)}, bf16[768,384]{1,0:T(8,128)(2,1)}, u32[]{:S(2)}) copy-start(bf16[768,384]{1,0:T(8,128)(2,1)} %get-tuple-element.170) | copy-start | bytes 1769476
  350.5 2.3 collective-permute-start.13
  350.6 3.9 collective-permute-start.15
  351.1 3.4 collective-permute-start.12
  351.2 3.9 collective-permute-start.14
  352.8 2.3 copy-start.14
  383.1 10.5 %collective-permute-start.17 = (bf16[2,4,4,48,768]{4,3,2,1,0:T(8,128)(2,1)}, bf16[2,4,4,48,768]{4,3,2,1,0:T(8,128)(2,1)S(1)}, u32[]{:S(2)}, u32[]{:S(2)}) collective-permute-start(bf16[2,4,4,48,768]{4,3,2,1,0:T(8,128)(2,1)} %get-tuple-element.180), channel_id=1, source_target_pairs={{0,1},{1,0},{2,3},{3,2},{4,5},{5,4},{6,7},{7,6},{8,9},{9,8},{10,11... | collective-permute-start | bytes 7077896 | tf_op jit(solution)/shard_map/ppermute | solution.py:1128
  414.1 18.1 %collective-permute-start.18 = (bf16[2,4,8,48,768]{4,3,2,1,0:T(8,128)(2,1)}, bf16[2,4,8,48,768]{4,3,2,1,0:T(8,128)(2,1)}, u32[]{:S(2)}, u32[]{:S(2)}) collective-permute-start(bf16[2,4,8,48,768]{4,3,2,1,0:T(8,128)(2,1)} %get-tuple-element.185), channel_id=1, source_target_pairs={{0,1},{1,0},{2,3},{3,2},{4,5},{5,4},{6,7},{7,6},{8,9},{9,8},{10,11... | collective-permute-start | bytes 14155784 | tf_op jit(solution)/shard_map/ppermute | solution.py:1128
  414.5 93.0 %reduce-scatter.7.cloned.1.call-start = ((), (), s32[]{:S(2)}) async-start(), calls=%async_computation.5 | async-start | bytes 1474560 | tf_op jit(solution)/shard_map/reduce_scatter | solution.py:1144
  415.4 42.1 %collective-permute-start.19 = (bf16[4,4,48,768]{3,2,1,0:T(8,128)(2,1)S(1)}, bf16[4,4,48,768]{3,2,1,0:T(8,128)(2,1)}, u32[]{:S(2)}, u32[]{:S(2)}) collective-permute-start(bf16[4,4,48,768]{3,2,1,0:T(8,128)(2,1)S(1)} %copy-done.24), channel_id=1, source_target_pairs={{0,2},{1,3},{2,0},{3,1},{4,6},{5,7},{6,4},{7,5},{8,10},{9,11},{10,... | collective-permute-start | bytes 3538952 | tf_op jit(solution)/shard_map/ppermute | solution.py:1136
  436.6 64.0 %collective-permute-start.26 = (bf16[4,8,48,768]{3,2,1,0:T(8,128)(2,1)}, bf16[4,8,48,768]{3,2,1,0:T(8,128)(2,1)S(1)}, u32[]{:S(2)}, u32[]{:S(2)}) collective-permute-start(bf16[4,8,48,768]{3,2,1,0:T(8,128)(2,1)} %sum_along.6.refs_10_), channel_id=1, source_target_pairs={{0,2},{1,3},{2,0},{3,1},{4,6},{5,7},{6,4},{7,5},{8,10},{9,11},{10,... | collective-permute-start | bytes 7077896 | tf_op jit(solution)/shard_map/ppermute | solution.py:1136
  461.6 112.1 %reduce-scatter.9.cloned.1.call-start = ((), (), s32[]{:S(2)}) async-start(), calls=%async_computation.6 | async-start | bytes 2949120 | tf_op jit(solution)/shard_map/reduce_scatter | solution.py:1144
  482.7 2.3 collective-permute-start.21
  482.8 3.7 collective-permute-start.23
  483.3 3.5 collective-permute-start.20
  483.3 4.3 collective-permute-start.22
  485.0 2.6 copy-start.26
  485.0 15.6 %collective-permute-start.25 = (bf16[8,48,768]{2,1,0:T(8,128)(2,1)}, bf16[8,48,768]{2,1,0:T(8,128)(2,1)S(1)}, u32[]{:S(2)}, u32[]{:S(2)}) collective-permute-start(bf16[8,48,768]{2,1,0:T(8,128)(2,1)} %bitcast.87), channel_id=1, source_target_pairs={{0,16},{16,0},{1,17},{17,1},{2,18},{18,2},{3,19},{19,3},{4,20},{20... | collective-permute-start | bytes 1769480 | tf_op jit(solution)/shard_map/ppermute | solution.py:1162
  507.4 78.5 %reduce-scatter.11.cloned.1.call-start = ((), (), s32[]{:S(2)}) async-start(), calls=%async_computation.7 | async-start | bytes 1474560 | tf_op jit(solution)/shard_map/reduce_scatter | solution.py:1144
  507.4 9.7 %collective-permute-start.24 = (bf16[2,4,4,48,768]{4,3,2,1,0:T(8,128)(2,1)}, bf16[2,4,4,48,768]{4,3,2,1,0:T(8,128)(2,1)S(1)}, u32[]{:S(2)}, u32[]{:S(2)}) collective-permute-start(bf16[2,4,4,48,768]{4,3,2,1,0:T(8,128)(2,1)} %get-tuple-element.199), channel_id=1, source_target_pairs={{0,1},{1,0},{2,3},{3,2},{4,5},{5,4},{6,7},{7,6},{8,9},{9,8},{10,11... | collective-permute-start | bytes 7077896 | tf_op jit(solution)/shard_map/ppermute | solution.py:1128
  507.6 9.6 %collective-permute-start.27 = (bf16[4,48,768]{2,1,0:T(8,128)(2,1)}, bf16[4,48,768]{2,1,0:T(8,128)(2,1)S(1)}, u32[]{:S(2)}, u32[]{:S(2)}) collective-permute-start(bf16[4,48,768]{2,1,0:T(8,128)(2,1)} %bitcast.96), channel_id=1, source_target_pairs={{0,16},{16,0},{1,17},{17,1},{2,18},{18,2},{3,19},{19,3},{4,20},{20... | collective-permute-start | bytes 884744 | tf_op jit(solution)/shard_map/ppermute | solution.py:1162
  522.3 27.9 %collective-permute-start.28 = (bf16[4,4,48,768]{3,2,1,0:T(8,128)(2,1)}, bf16[4,4,48,768]{3,2,1,0:T(8,128)(2,1)S(1)}, u32[]{:S(2)}, u32[]{:S(2)}) collective-permute-start(bf16[4,4,48,768]{3,2,1,0:T(8,128)(2,1)} %sum_along.7.refs_14_), channel_id=1, source_target_pairs={{0,2},{1,3},{2,0},{3,1},{4,6},{5,7},{6,4},{7,5},{8,10},{9,11},{10,... | collective-permute-start | bytes 3538952 | tf_op jit(solution)/shard_map/ppermute | solution.py:1136
  557.9 1.5 collective-permute-start.29
  560.3 4.2 collective-permute-start.30
  568.0 14.5 %collective-permute-start.31 = (bf16[384,768]{1,0:T(8,128)(2,1)}, bf16[384,768]{1,0:T(8,128)(2,1)S(1)}, u32[]{:S(2)}, u32[]{:S(2)}) collective-permute-start(bf16[384,768]{1,0:T(8,128)(2,1)} %get-tuple-element.214), channel_id=1, source_target_pairs={{0,2},{1,3},{2,0},{3,1},{4,6},{5,7},{6,4},{7,5},{8,10},{9,11},{10,... | collective-permute-start | bytes 1769480 | tf_op jit(solution)/shard_map/ppermute | solution.py:1070
  569.7 5.5 copy-start.31
  573.7 14.2 %collective-permute-start.34 = (bf16[8,48,768]{2,1,0:T(8,128)(2,1)}, bf16[8,48,768]{2,1,0:T(8,128)(2,1)S(1)}, u32[]{:S(2)}, u32[]{:S(2)}) collective-permute-start(bf16[8,48,768]{2,1,0:T(8,128)(2,1)} %bitcast.84), channel_id=1, source_target_pairs={{0,16},{16,0},{1,17},{17,1},{2,18},{18,2},{3,19},{19,3},{4,20},{20... | collective-permute-start | bytes 1769480 | tf_op jit(solution)/shard_map/ppermute | solution.py:1162
  575.2 18.1 %collective-permute-start.35 = (f32[24,128]{1,0:T(8,128)S(1)}, f32[24,128]{1,0:T(8,128)S(1)}, u32[]{:S(2)}, u32[]{:S(2)}) collective-permute-start(f32[24,128]{1,0:T(8,128)S(1)} %get-tuple-element.283), channel_id=1, source_target_pairs={{0,4},{4,8},{8,12},{12,0},{1,5},{5,9},{9,13},{13,1},{2,6},{6,10},{... | collective-permute-start | bytes 36872 | tf_op jit(solution)/shard_map/ppermute | solution.py:1386
  575.6 17.8 %collective-permute-start.36 = (f32[24,128]{1,0:T(8,128)S(1)}, f32[24,128]{1,0:T(8,128)S(1)}, u32[]{:S(2)}, u32[]{:S(2)}) collective-permute-start(f32[24,128]{1,0:T(8,128)S(1)} %get-tuple-element.282), channel_id=1, source_target_pairs={{0,8},{4,12},{8,0},{12,4},{1,9},{5,13},{9,1},{13,5},{2,10},{6,14},... | collective-permute-start | bytes 36872 | tf_op jit(solution)/shard_map/ppermute | solution.py:1386
  576.5 7.6 %copy-start.27 = (bf16[384,768]{1,0:T(8,128)(2,1)S(1)}, bf16[384,768]{1,0:T(8,128)(2,1)}, u32[]{:S(2)}) copy-start(bf16[384,768]{1,0:T(8,128)(2,1)} %get-tuple-element.213) | copy-start | bytes 1769476
  576.5 16.8 %collective-permute-start.37 = (f32[24,128]{1,0:T(8,128)S(1)}, f32[24,128]{1,0:T(8,128)S(1)}, u32[]{:S(2)}, u32[]{:S(2)}) collective-permute-start(f32[24,128]{1,0:T(8,128)S(1)} %get-tuple-element.281), channel_id=1, source_target_pairs={{0,12},{4,0},{8,4},{12,8},{1,13},{5,1},{9,5},{13,9},{2,14},{6,2},{... | collective-permute-start | bytes 36872 | tf_op jit(solution)/shard_map/ppermute | solution.py:1386
  582.4 13.6 %collective-permute-start.32 = (bf16[384,768]{1,0:T(8,128)(2,1)}, bf16[384,768]{1,0:T(8,128)(2,1)S(1)}, u32[]{:S(2)}, u32[]{:S(2)}) collective-permute-start(bf16[384,768]{1,0:T(8,128)(2,1)} %get-tuple-element.224), channel_id=1, source_target_pairs={{0,2},{1,3},{2,0},{3,1},{4,6},{5,7},{6,4},{7,5},{8,10},{9,11},{10,... | collective-permute-start | bytes 1769480 | tf_op jit(solution)/shard_map/ppermute | solution.py:1070
  587.9 8.1 %copy-start.23 = (f32[384,768]{1,0:T(8,128)S(1)}, f32[384,768]{1,0:T(8,128)}, u32[]{:S(2)}) copy-start(f32[384,768]{1,0:T(8,128)} %get-tuple-element.223) | copy-start | bytes 3538948
  587.9 13.8 %collective-permute-start.33 = (bf16[4,48,768]{2,1,0:T(8,128)(2,1)}, bf16[4,48,768]{2,1,0:T(8,128)(2,1)S(1)}, u32[]{:S(2)}, u32[]{:S(2)}) collective-permute-start(bf16[4,48,768]{2,1,0:T(8,128)(2,1)} %bitcast.91), channel_id=1, source_target_pairs={{0,16},{16,0},{1,17},{17,1},{2,18},{18,2},{3,19},{19,3},{4,20},{20... | collective-permute-start | bytes 884744 | tf_op jit(solution)/shard_map/ppermute | solution.py:1162
  593.4 13.1 %collective-permute-start.38 = (bf16[2,12,48]{2,1,0:T(8,128)(2,1)S(1)}, bf16[2,12,48]{2,1,0:T(8,128)(2,1)S(1)}, u32[]{:S(2)}, u32[]{:S(2)}) collective-permute-start(bf16[2,12,48]{2,1,0:T(8,128)(2,1)S(1)} %convert_element_type.43), channel_id=1, source_target_pairs={{0,16},{16,0},{1,17},{17,1},{2,18},{18,2},{3,19},{19,3},{4,20},{20... | collective-permute-start | bytes 6920 | tf_op jit(solution)/shard_map/ppermute | solution.py:1421
  602.5 4.0 copy-start.32
  602.5 4.0 copy-start.33
  602.5 4.0 copy-start.34
  (19 other events, 21.6 us)
Sparse Core Ops, SparseCore 0:
  11.8 89.9 all-gather.6
  104.6 79.6 all-gather.4
  414.7 46.7 reduce-scatter.4
  464.2 28.6 reduce-scatter.6
  507.5 46.6 reduce-scatter.8
  556.4 29.4 reduce-scatter.10
